TPU v7x, 32 devices: a whole 2x2x4 slice. The times are simulated.
32 devices in a mesh: dp: 4 (over y, x), expert: 8 (over z, core).
Axes of the slice: x: 2, y: 2, z: 4, core: 2. Of those that a mesh axis runs over, the one named last changes fastest.
Arguments:
- tokens: bfloat16 [4096, 2560], P(('dp', 'expert')), may hold values from -6 to 6
- cotangent: bfloat16 [4096, 2560], P(('dp', 'expert')), may hold values from -6 to 6
- routes: int32 [4096, 2], P(('dp', 'expert')), may hold values from 0 to 3, all different within a row; in each aligned block of 128 rows (0 to 127, 128 to 255, ...) at most 80 rows name the same one
- gate_values: float32 [4096, 2], P(('dp', 'expert')), may hold values from 0.1 to 1
- up_weight: bfloat16 [8, 2560, 384], P('expert', 'dp'), may hold values from -0.125 to 0.125
- down_weight: bfloat16 [8, 2560, 384], P('expert', 'dp'), may hold values from -0.21875 to 0.21875
Outputs:
- grad_tokens: bfloat16 [4096, 2560], P(('dp', 'expert'))
- grad_up: bfloat16 [8, 2560, 384], P('expert', 'dp')
- grad_down: bfloat16 [8, 2560, 384], P('expert', 'dp')
Inputs may be any that keep to these rules, and one draw needn't show every extreme that they name: `routes`: each row names 2 different experts. Among the rows of one device no expert is named by more than 80 rows, a bound that some block reaches.
All inputs are finite; a program needn't handle non-finite values.
Results may differ from a plain program's by a relative error of at most 0.023.
Values may be sent and summed in bfloat16 or wider, within the bound.
No kernel may reach another device: no remote copies, remote signals or barrier semaphores. Data moves between devices by JAX's collectives and lax.ppermute only.
A program may use at most 64 MiB of HBM per device.

v0:
```python
import jax
import jax.numpy as jnp
from jax import lax
from jax.sharding import PartitionSpec as P


def activation(hidden):
    sigmoid_h = jax.nn.sigmoid(hidden)
    return (hidden * sigmoid_h, sigmoid_h * (1.0 + hidden * (1.0 - sigmoid_h)))


def on_device(tokens, cotangent, routes, gate_values, up_weight, down_weight):
    tok_rows, model_width = tokens.shape
    top_count = routes.shape[1]
    slot_count = lax.axis_size("expert")
    experts = slot_count // 2
    capacity = 5 * tok_rows * top_count // (4 * experts)
    flat_routes = routes.reshape(-1)
    onehot = (flat_routes[:, None] == jnp.arange(experts, dtype=jnp.int32)[None, :]).astype(
        jnp.int32
    )
    position = jnp.sum((jnp.cumsum(onehot, axis=0) - onehot) * onehot, axis=1)
    slot_index = flat_routes * capacity + position
    owners = jnp.arange(tok_rows * top_count, dtype=jnp.int32) // top_count
    row_table = jnp.full((experts * capacity,), tok_rows, jnp.int32).at[slot_index].set(owners)
    gate_table = (
        jnp.zeros((experts * capacity,), jnp.float32).at[slot_index].set(gate_values.reshape(-1))
    )
    zero_row = jnp.zeros((1, model_width), jnp.bfloat16)
    send_x = jnp.concatenate([tokens, zero_row])[row_table]
    send_s = (
        gate_table[:, None] * jnp.concatenate([cotangent, zero_row])[row_table].astype(jnp.float32)
    ).astype(jnp.bfloat16)
    shaped_x = send_x.reshape(experts, 1, capacity, model_width)
    shaped_s = send_s.reshape(experts, 1, capacity, model_width)
    doubled_x = jnp.broadcast_to(shaped_x, (experts, 2, capacity, model_width)).reshape(
        slot_count, capacity, model_width
    )
    doubled_s = jnp.broadcast_to(shaped_s, (experts, 2, capacity, model_width)).reshape(
        slot_count, capacity, model_width
    )
    landed_x, landed_s = (
        lax.all_to_all(doubled_x, "expert", split_axis=0, concat_axis=0, tiled=True),
        lax.all_to_all(doubled_s, "expert", split_axis=0, concat_axis=0, tiled=True),
    )
    weight_up, weight_down = (
        lax.all_gather(up_weight, "dp", axis=1, tiled=True),
        lax.all_gather(down_weight, "dp", axis=1, tiled=True),
    )
    weight_up = weight_up[0]
    weight_down = weight_down[0]
    rows_x = landed_x.reshape(-1, model_width)
    rows_s = landed_s.reshape(-1, model_width)
    hidden = jnp.dot(rows_x, weight_up, preferred_element_type=jnp.float32)
    active, slope_term = activation(hidden)
    active = active.astype(jnp.bfloat16)
    back_act = jnp.dot(rows_s, weight_down, preferred_element_type=jnp.float32)
    back_hidden = (back_act * slope_term).astype(jnp.bfloat16)
    partial_value = lax.dot_general(
        back_hidden, weight_up, (((1,), (1,)), ((), ())), preferred_element_type=jnp.float32
    ).astype(jnp.bfloat16)
    by_source = partial_value.reshape(slot_count, capacity, model_width)
    returned = lax.all_to_all(by_source, "expert", split_axis=0, concat_axis=0, tiled=True)
    flat_back = returned.reshape(slot_count * capacity, model_width)
    first_index = 2 * flat_routes * capacity + position
    paired = (
        flat_back[first_index].astype(jnp.float32)
        + flat_back[first_index + capacity].astype(jnp.float32)
    ).astype(jnp.bfloat16)
    paired = lax.optimization_barrier(paired)
    grad_tokens = jnp.sum(
        paired.astype(jnp.float32).reshape(tok_rows, top_count, model_width), axis=1
    ).astype(jnp.bfloat16)
    term_up = lax.dot_general(
        rows_x, back_hidden, (((0,), (0,)), ((), ())), preferred_element_type=jnp.float32
    )
    term_down = lax.dot_general(
        rows_s, active, (((0,), (0,)), ((), ())), preferred_element_type=jnp.float32
    )
    reduced = lax.psum_scatter(
        jnp.concatenate([term_up, term_down], axis=1).astype(jnp.bfloat16),
        "dp",
        scatter_dimension=0,
        tiled=True,
    ).astype(jnp.float32)
    half_width = weight_up.shape[1]
    grad_up = reduced[:, :half_width].astype(jnp.bfloat16)[None]
    grad_down = reduced[:, half_width:].astype(jnp.bfloat16)[None]
    return (grad_tokens, grad_up, grad_down)


def solution(mesh):
    in_specs = (
        P(("dp", "expert"), None),
        P(("dp", "expert"), None),
        P(("dp", "expert"), None),
        P(("dp", "expert"), None),
        P("expert", "dp", None),
        P("expert", "dp", None),
    )
    out_specs = (P(("dp", "expert"), None), P("expert", "dp", None), P("expert", "dp", None))
    return jax.shard_map(
        on_device, mesh=mesh, in_specs=in_specs, out_specs=out_specs, check_vma=False
    )
```

profile of v0, /device:TPU:9, one launch (start us, length us, event | category | flops | bytes accessed | tf_op | source)
XLA Modules:
  0.0 301.4 jit_solution(8814021361816044353)
XLA Ops:
  7.2 0.8 copy.23
  8.0 0.1 eq.29
  8.1 0.1 eq.25
  8.2 0.7 broadcast_multiply_fusion
  8.9 1.2 reduce-window.6
  10.1 0.1 slice.26
  10.2 0.1 copy.25
  10.4 0.1 copy.26
  10.5 0.1 add_bitcast_fusion
  10.5 0.1 copy.22
  10.7 0.1 mul.64
  10.8 0.1 copy.28
  10.9 0.1 mul.74
  11.1 1.4 scatter_custom_fusion.1
  12.5 1.1 concatenate.11
  13.7 2.6 gather_fusion.1
  16.3 2.0 broadcast_in_dim.40
  18.2 0.0 copy-start.1
  18.2 5.8 %all-to-all-start.1 = ((bf16[8,80,2560]{2,1,0:T(8,128)(2,1)}), bf16[8,80,2560]{2,1,0:T(8,128)(2,1)}, u32[]{:S(2)}, u32[]{:S(2)}) async-start(bf16[8,80,2560]{2,1,0:T(8,128)(2,1)} %bitcast.9), calls=%async_computation.1 | async-start | bytes 6553600 | tf_op jit(solution)/shard_map/all_to_all | solution.py:43
  24.0 0.0 copy-done.1
  24.1 0.0 copy-start.2
  24.1 2.6 gather_fusion
  26.7 0.0 copy-done.2
  26.7 0.1 copy.27
  26.8 0.1 reshape.194
  26.9 1.4 scatter_custom_fusion
  28.3 0.1 mul.66
  28.4 0.3 fusion
  28.8 66.0 %all-to-all-done.1 = bf16[8,80,2560]{2,1,0:T(8,128)(2,1)} async-done(((bf16[8,80,2560]{2,1,0:T(8,128)(2,1)}), bf16[8,80,2560]{2,1,0:T(8,128)(2,1)}, u32[]{:S(2)}, u32[]{:S(2)}) %all-to-all-start.1) | async-done | bytes 3276832 | tf_op jit(solution)/shard_map/all_to_all | solution.py:43
  94.8 2.0 broadcast_in_dim.38
  96.8 7.2 %all-to-all-start = ((bf16[8,80,2560]{2,1,0:T(8,128)(2,1)}), bf16[8,80,2560]{2,1,0:T(8,128)(2,1)S(1)}, u32[]{:S(2)}, u32[]{:S(2)}) async-start(bf16[8,80,2560]{2,1,0:T(8,128)(2,1)} %bitcast.5), calls=%async_computation | async-start | bytes 6553600 | tf_op jit(solution)/shard_map/all_to_all | solution.py:44
  104.0 0.0 all-gather.5.cloned.1.call-start
  104.0 0.7 all-gather.5.cloned.1.call-update
  104.7 0.0 all-gather.3.cloned.1.call-start
  104.8 0.7 all-gather.3.cloned.1.call-update
  105.5 0.2 reduce-scatter.4.cloned.1.call-start
  105.7 35.9 %all-gather.5.cloned.1.call-done = bf16[1,2560,384]{2,1,0:T(8,128)(2,1)} async-done(((bf16[1,640,384]{2,1,0:T(8,128)(2,1)}), bf16[1,2560,384]{2,1,0:T(8,128)(2,1)}) %all-gather.5.cloned.1.call-update) | async-done | bytes 1966096 | tf_op jit(solution)/shard_map/all_gather | solution.py:47
  141.6 5.3 %fusion.2 = f32[640,384]{1,0:T(8,128)} fusion(bf16[640,2560]{1,0:T(8,128)(2,1)} %bitcast.10, bf16[1,2560,384]{2,1,0:T(8,128)(2,1)} %all-gather.5.cloned.1.call-done), kind=kOutput, calls=%fused_computation.14 | convolution fusion | flops 1258291200 | bytes 6225920 | tf_op jit(solution)/shard_map/dot_general | solution.py:54
  146.9 27.9 %all-to-all-done = bf16[8,80,2560]{2,1,0:T(8,128)(2,1)S(1)} async-done(((bf16[8,80,2560]{2,1,0:T(8,128)(2,1)}), bf16[8,80,2560]{2,1,0:T(8,128)(2,1)S(1)}, u32[]{:S(2)}, u32[]{:S(2)}) %all-to-all-start) | async-done | bytes 3276832 | tf_op jit(solution)/shard_map/all_to_all | solution.py:44
  174.8 4.3 %convolution_convert_fusion.1 = bf16[2560,384]{0,1:T(8,128)(2,1)} fusion(bf16[640,2560]{1,0:T(8,128)(2,1)S(1)} %bitcast.57, f32[640,384]{1,0:T(8,128)} %fusion.2), kind=kOutput, calls=%fused_computation.7 | convolution fusion | flops 1260503040 | bytes 6225920 | tf_op jit(solution)/shard_map/dot_general | solution.py:77
  179.1 0.0 all-gather.3.cloned.1.call-done
  179.1 3.7 %fusion.9 = bf16[640,384]{1,0:T(8,128)(2,1)S(1)} fusion(bf16[640,2560]{1,0:T(8,128)(2,1)S(1)} %bitcast.58, bf16[1,2560,384]{2,1,0:T(8,128)(2,1)} %all-gather.3.cloned.1.call-done, f32[640,384]{1,0:T(8,128)} %fusion.2), kind=kOutput, calls=%fused_computation.19 | convolution fusion | flops 1260503040 | bytes 6717440 | tf_op jit(solution)/shard_map/dot_general | solution.py:57
  182.8 0.0 copy-start.4
  182.9 0.8 copy-done.4
  183.6 3.8 %convolution_convert_fusion.2 = bf16[2560,384]{0,1:T(8,128)(2,1)S(1)} fusion(bf16[640,2560]{1,0:T(8,128)(2,1)} %bitcast.10, bf16[640,384]{1,0:T(8,128)(2,1)S(1)} %fusion.9), kind=kOutput, calls=%fused_computation.8 | convolution fusion | flops 1259274240 | bytes 5734400 | tf_op jit(solution)/shard_map/dot_general | solution.py:74
  187.4 0.0 copy-done
  187.4 2.2 pad_maximum_fusion
  189.6 6.3 %copy.31 = bf16[2560,768]{1,0:T(8,128)(2,1)} copy(bf16[2560,768]{0,1:T(8,128)(2,1)} %pad_maximum_fusion) | data formatting | bytes 7864320
  196.0 0.0 reduce-scatter.4.cloned.1.call-update
  196.0 1.5 copy-done.3
  197.5 0.1 copy-done.5
  197.6 3.6 %convolution_convert_fusion = bf16[640,2560]{1,0:T(8,128)(2,1)} fusion(bf16[640,384]{1,0:T(8,128)(2,1)S(1)} %copy-done.5, bf16[1,2560,384]{2,1,0:T(8,128)(2,1)S(1)} %copy-done.3), kind=kOutput, calls=%fused_computation.6 | convolution fusion | flops 1259929600 | bytes 5734400 | tf_op jit(solution)/shard_map/dot_general | solution.py:59
  201.2 7.1 %all-to-all-start.2 = ((bf16[8,80,2560]{2,1,0:T(8,128)(2,1)}), bf16[8,80,2560]{2,1,0:T(8,128)(2,1)S(1)}, u32[]{:S(2)}, u32[]{:S(2)}) async-start(bf16[8,80,2560]{2,1,0:T(8,128)(2,1)} %bitcast.59), calls=%async_computation.2 | async-start | bytes 6553600 | tf_op jit(solution)/shard_map/all_to_all | solution.py:63
  208.4 70.8 %all-to-all-done.2 = bf16[8,80,2560]{2,1,0:T(8,128)(2,1)S(1)} async-done(((bf16[8,80,2560]{2,1,0:T(8,128)(2,1)}), bf16[8,80,2560]{2,1,0:T(8,128)(2,1)S(1)}, u32[]{:S(2)}, u32[]{:S(2)}) %all-to-all-start.2) | async-done | bytes 3276832 | tf_op jit(solution)/shard_map/all_to_all | solution.py:63
  279.2 2.5 gather_fusion.2
  281.7 2.5 gather_fusion.3
  284.2 2.0 add_convert_fusion
  286.2 0.5 reshape.155
  286.7 4.4 %reduce = bf16[128,2560]{1,0:T(8,128)(2,1)} reduce(bf16[128,2,2560]{2,1,0:T(2,128)(2,1)S(1)} %reshape.155, bf16[]{:T(256)} %constant.36.clone.1), dimensions={1}, to_apply=%region_5.6.clone | reduce | flops 327680 | bytes 1966082 | tf_op jit(solution)/shard_map/reduce_sum | solution.py:71
  291.1 1.3 fusion.21
  292.4 0.3 copy.33
  292.6 1.0 copy.29
  293.6 0.3 copy.34
  293.9 1.0 copy.30
  (15 shorter events, 0.2 us)
Async XLA Ops:
  18.2 5.8 %copy-start.1 = (bf16[128,2560]{1,0:T(8,128)(2,1)S(1)}, bf16[128,2560]{1,0:T(8,128)(2,1)}, u32[]{:S(2)}) copy-start(bf16[128,2560]{1,0:T(8,128)(2,1)} %param.7) | copy-start | bytes 1966084
  18.2 76.6 %all-to-all-start.1 = ((bf16[8,80,2560]{2,1,0:T(8,128)(2,1)}), bf16[8,80,2560]{2,1,0:T(8,128)(2,1)}, u32[]{:S(2)}, u32[]{:S(2)}) async-start(bf16[8,80,2560]{2,1,0:T(8,128)(2,1)} %bitcast.9), calls=%async_computation.1 | async-start | bytes 6553600 | tf_op jit(solution)/shard_map/all_to_all | solution.py:43
  24.1 2.6 copy-start.2
  96.8 78.0 %all-to-all-start = ((bf16[8,80,2560]{2,1,0:T(8,128)(2,1)}), bf16[8,80,2560]{2,1,0:T(8,128)(2,1)S(1)}, u32[]{:S(2)}, u32[]{:S(2)}) async-start(bf16[8,80,2560]{2,1,0:T(8,128)(2,1)} %bitcast.5), calls=%async_computation | async-start | bytes 6553600 | tf_op jit(solution)/shard_map/all_to_all | solution.py:44
  104.0 37.6 %all-gather.5.cloned.1.call-start = ((), (), s32[]{:S(2)}) async-start(), calls=%async_computation.5 | async-start | bytes 2457600 | tf_op jit(solution)/shard_map/all_gather | solution.py:47
  104.7 74.3 %all-gather.3.cloned.1.call-start = ((), (), s32[]{:S(2)}) async-start(), calls=%async_computation.4 | async-start | bytes 2457600 | tf_op jit(solution)/shard_map/all_gather | solution.py:48
  105.5 185.6 %reduce-scatter.4.cloned.1.call-start = ((), (), s32[]{:S(2)}) async-start(), calls=%async_computation.6 | async-start | bytes 4915200
  182.8 0.8 copy-start.4
  183.6 3.8 %copy-start = (bf16[2560,384]{0,1:T(8,128)(2,1)S(1)}, bf16[2560,384]{0,1:T(8,128)(2,1)}, u32[]{:S(2)}) copy-start(bf16[2560,384]{0,1:T(8,128)(2,1)} %convolution_convert_fusion.1) | copy-start | bytes 5898244
  196.0 1.5 copy-start.3
  196.0 1.6 copy-start.5
  201.2 77.9 %all-to-all-start.2 = ((bf16[8,80,2560]{2,1,0:T(8,128)(2,1)}), bf16[8,80,2560]{2,1,0:T(8,128)(2,1)S(1)}, u32[]{:S(2)}, u32[]{:S(2)}) async-start(bf16[8,80,2560]{2,1,0:T(8,128)(2,1)} %bitcast.59), calls=%async_computation.2 | async-start | bytes 6553600 | tf_op jit(solution)/shard_map/all_to_all | solution.py:63
Sparse Core Ops, SparseCore 0:
  106.7 34.8 all-gather.4
  143.5 34.2 all-gather.2
  196.1 52.1 reduce-scatter.3
where the time goes:
time: 306 us; the launch traced here: 301 us
  waiting for transfers between devices  202 us (66%)
  local copies, waits for them, and re-layouts  33.3 us (11%)
  matrix products  20.8 us (7%)
  starting transfers between devices  20.4 us (7%)
  between operations  13.9 us (5%)
  other arithmetic  11 us (4%)
    all_to_all x1, waiting for transfers between devices, on_device(): lax.all_to_all(by_source, 'expert', split_axis=0, concat_axis=0, tiled=True)  70.8 us
    all_to_all x1, waiting for transfers between devices, on_device(): lax.all_to_all(doubled_x, 'expert', split_axis=0, concat_axis=0, tiled=True)  66 us
    all_gather x1, waiting for transfers between devices, on_device(): lax.all_gather(up_weight, 'dp', axis=1, tiled=True)  35.9 us
    all_to_all x1, waiting for transfers between devices, on_device(): lax.all_to_all(doubled_s, 'expert', split_axis=0, concat_axis=0, tiled=True)  27.9 us
    unnamed x19, local copies, waits for them, and re-layouts  12.1 us
    all_to_all x1, starting transfers between devices, on_device(): lax.all_to_all(doubled_s, 'expert', split_axis=0, concat_axis=0, tiled=True)  7.23 us
    all_to_all x1, starting transfers between devices, on_device(): lax.all_to_all(by_source, 'expert', split_axis=0, concat_axis=0, tiled=True)  7.15 us
  transfers between devices with their start and end apart: 6, of which 4 were waited for; matrix products, arithmetic and copies ran while one was open for 10% of the time, Pallas kernels for 0%

commit v1 on v0

v1 whole, which is shorter than its diff:
```python
import functools

import jax
import jax.numpy as jnp
from jax import lax
from jax.experimental import pallas as pl
from jax.experimental.pallas import tpu as pltpu
from jax.sharding import PartitionSpec as P

BF = jnp.bfloat16
F32 = jnp.float32
MIB = 1024 * 1024


def vmem():
    return pl.BlockSpec(memory_space=pltpu.VMEM)


def hbm():
    return pl.BlockSpec(memory_space=pl.ANY)


def params(mebibytes):
    return pltpu.CompilerParams(vmem_limit_bytes=mebibytes * MIB)


def cost(microseconds):
    return pl.CostEstimate(
        flops=int(microseconds * 1.0e9), bytes_accessed=2**20, transcendentals=0
    )


def array(*shape):
    return jax.ShapeDtypeStruct(shape, BF)


def contract(a, b, da, db):
    return lax.dot_general(a, b, (((da,), (db,)), ((), ())), preferred_element_type=F32)


def slot_plan(routes):
    tokens = routes.shape[1]
    first, second = routes[0:1, :], routes[1:2, :]
    expert = lax.broadcasted_iota(jnp.int32, (128, tokens), 0)
    named = jnp.where((expert == first) | (expert == second), 1.0, 0.0).astype(BF)
    earlier = lax.broadcasted_iota(jnp.int32, (tokens, tokens), 0)
    later = lax.broadcasted_iota(jnp.int32, (tokens, tokens), 1)
    place = contract(named, jnp.where(earlier < later, 1.0, 0.0).astype(BF), 1, 0)
    return first, second, expert, place


def slot_masks(plan, chosen, cap):
    first, second, expert, place = plan
    own = jnp.sum(jnp.where(expert == chosen, place, 0.0), axis=0, keepdims=True)
    slot = lax.broadcasted_iota(jnp.int32, (cap, first.shape[1]), 0)
    here = slot == own.astype(jnp.int32)
    return here & (first == chosen), here & (second == chosen)


def dispatch_kernel(experts, cap, shifts, moved, *refs):
    refs = list(refs)
    sources, refs = refs[: 4 + moved], refs[4 + moved :]
    moved_outs, outs, refs = refs[:moved], refs[moved : moved + len(shifts)], refs[moved + len(shifts) :]
    routes_ref, gates_ref, tok_ref, cot_ref, made, held, sems = refs
    landings = [routes_ref, gates_ref, tok_ref, cot_ref] + [held.at[i] for i in range(moved)]
    copies = []

    def copy(source, landing):
        copies.append(pltpu.make_async_copy(source, landing, sems.at[len(copies)]))
        copies[-1].start()

    for source, landing in zip(sources, landings):
        copy(source, landing)
    for one in copies[:2]:
        one.wait()
    chip = lax.axis_index("expert") // 2
    plan = slot_plan(routes_ref[...])
    gates = gates_ref[...]
    for one in copies[2:4]:
        one.wait()
    for index, shift in enumerate(shifts):
        mask0, mask1 = slot_masks(plan, lax.rem(chip + shift, experts), cap)
        gate = jnp.sum(
            jnp.where(mask0, gates[0:1, :], 0.0) + jnp.where(mask1, gates[1:2, :], 0.0),
            axis=1,
            keepdims=True,
        )
        pick = jnp.where(mask0 | mask1, 1.0, 0.0).astype(BF)
        made[index, :cap, :] = contract(pick, tok_ref[...], 1, 0).astype(BF)
        made[index, cap:, :] = (gate * contract(pick, cot_ref[...], 1, 0)).astype(BF)
        copy(made.at[index], outs[index])
    for index in range(moved):
        copies[4 + index].wait()
        copy(held.at[index], moved_outs[index])
    for one in copies[4 + moved :]:
        one.wait()


def combine_kernel(experts, cap, routes_ref, *rest):
    backs, out_ref, mark_ref = rest[:-2], rest[-2], rest[-1]
    mark_ref[...] = jnp.zeros_like(mark_ref)
    chip = lax.axis_index("expert") // 2
    plan = slot_plan(routes_ref[...])
    picks = []
    for shift in range(experts):
        mask0, mask1 = slot_masks(plan, lax.rem(chip + shift, experts), cap)
        picks.append(jnp.where(mask0 | mask1, 1.0, 0.0).astype(BF).T)
    width = out_ref.shape[1]
    tile = 640
    for start in range(0, width, tile):
        cols = slice(start, start + tile)
        total = None
        for shift in range(experts):
            term = contract(picks[shift], backs[shift][:, cols], 1, 0)
            total = term if total is None else total + term
        out_ref[:, cols] = total.astype(BF)


def chunk_rows(cap, owns, sibs, rows_x, rows_s):
    for index, block in enumerate(list(owns) + list(sibs)):
        place = slice(index * cap, (index + 1) * cap)
        rows_x[place, :] = block[:cap, :]
        rows_s[place, :] = block[cap:, :]


def expert_work(rows_x, rows_s, up, down):
    hidden = contract(rows_x[...], up[...], 1, 0)
    sig = jax.nn.sigmoid(hidden)
    active = (hidden * sig).astype(BF)
    slope = sig * (1.0 + hidden * (1.0 - sig))
    back_hidden = (contract(rows_s[...], down[...], 1, 0) * slope).astype(BF)
    return active, back_hidden


def tiles(width):
    tile = 512 if width % 512 == 0 else 128
    return [slice(start, start + tile) for start in range(0, width, tile)]


def partial_rows(back_hidden, up_turned, part_own, part_sib):
    half_rows = part_own.shape[0]
    for cols in tiles(part_own.shape[1]):
        part = contract(back_hidden, up_turned[:, cols], 1, 0).astype(BF)
        part_own[:, cols] = part[:half_rows]
        part_sib[:, cols] = part[half_rows:]


def first_kernel(cap, count, layout, n_dp, *refs):
    owns, sibs, refs = refs[:count], refs[count : 2 * count], refs[2 * count :]
    n_up, n_down = len(layout[0]), len(layout[1])
    ups, downs = refs[:n_up], refs[n_up : n_up + n_down]
    part_own, part_sib, grads, up, up_turned, down, rows_x, rows_s = refs[n_up + n_down :]
    step, half = ups[0].shape
    me = lax.axis_index("dp")
    for full, lay, blocks in ((up, layout[0], ups), (down, layout[1], downs)):
        for peers, block in zip(lay, blocks):
            for place, peer in enumerate(peers):
                home = pl.ds(pl.multiple_of((me ^ peer) * step, 16), step)
                full[home, :] = block[place * step : (place + 1) * step, :]
    up_turned[...] = up[...].T
    chunk_rows(cap, owns, sibs, rows_x, rows_s)
    active, back_hidden = expert_work(rows_x, rows_s, up, down)
    for base, units, rows in ((0, back_hidden, rows_x), (half, active, rows_s)):
        turned = units.T
        for owner in range(n_dp):
            cols = slice(owner * step, (owner + 1) * step)
            grads[owner, base : base + half, :] = contract(turned, rows[:, cols], 1, 0).astype(BF)
    partial_rows(back_hidden, up_turned, part_own, part_sib)


def late_kernel(cap, count, n_dp, named, *refs):
    owns, sibs, refs = refs[:count], refs[count : 2 * count], refs[2 * count :]
    up, up_turned, down = refs[:3]
    refs = refs[3 + named :]
    part_own, part_sib, outs = refs[0], refs[1], refs[2 : 2 + n_dp]
    rows_x, rows_s = refs[2 + n_dp :]
    half = up_turned.shape[0]
    step = (outs[0].shape[1] - 4 * half) // 2
    rows = outs[0].shape[0]
    me = lax.axis_index("dp")
    chunk_rows(cap, owns, sibs, rows_x, rows_s)
    active, back_hidden = expert_work(rows_x, rows_s, up, down)
    for peer, out in enumerate(outs):
        cols = pl.ds(pl.multiple_of((me ^ peer) * step, 128), step)
        out[:, :step] = rows_x[:rows, cols]
        out[:, step : 2 * step] = rows_s[:rows, cols]
        first = 2 * step
        for units in (back_hidden, active):
            for place in (slice(0, rows), slice(rows, 2 * rows)):
                out[:, first : first + half] = units[place]
                first += half
    partial_rows(back_hidden, up_turned, part_own, part_sib)


def pair_kernel(cap, counts, *refs):
    outs = refs[len(refs) - sum(counts) :]
    place = 0
    for group, count in enumerate(counts):
        own_ref, other_ref = refs[2 * group : 2 * group + 2]
        for index in range(count):
            rows = slice(index * cap, (index + 1) * cap)
            outs[place][...] = (
                own_ref[rows, :].astype(F32) + other_ref[rows, :].astype(F32)
            ).astype(BF)
            place += 1


def pass_kernel(*refs):
    pass


def share_kernel(*refs):
    blocks, out = refs[:-1], refs[-1]
    rows = blocks[0].shape[0]
    for index, block in enumerate(blocks):
        out[index * rows : (index + 1) * rows, :] = block[:, : out.shape[1]]


def last_kernel(n_dp, *refs):
    near, blocks, shared = refs[0], refs[1 : 1 + n_dp], refs[1 + n_dp]
    out_up, out_down, rows, units = refs[-4:]
    step, half = rows.shape[1], units.shape[1]
    count = blocks[0].shape[0]
    for base, out in ((0, out_up), (1, out_down)):
        cols = slice(base * step, (base + 1) * step)
        first = 2 * step + 2 * base * half
        for index, block in enumerate(blocks):
            place = slice(2 * index * count, (2 * index + 1) * count)
            rows[place, :] = block[:, cols]
            units[place, :] = block[:, first : first + half]
            place = slice((2 * index + 1) * count, (2 * index + 2) * count)
            rows[place, :] = shared[index * count : (index + 1) * count, cols]
            units[place, :] = block[:, first + half : first + 2 * half]
        total = contract(units[...].T, rows[...], 1, 0)
        total = total + near[base * half : (base + 1) * half, :].astype(F32)
        out[0] = total.T.astype(BF)


def on_device(n_dp, n_expert, tokens, cotangent, routes, gate_values, up_weight, down_weight):
    rows, width = tokens.shape
    top = routes.shape[1]
    experts = n_expert // 2
    cap = -(-(5 * rows * top // (4 * experts)) // 16) * 16
    step, half = up_weight.shape[1:]
    bits = n_dp.bit_length() - 1
    orders = (list(range(bits)), list(range(bits))[::-1])

    def shifted(value, shift):
        pairs = [
            (2 * z + c, 2 * ((z + shift) % experts) + c) for z in range(experts) for c in range(2)
        ]
        return lax.ppermute(value, "expert", pairs)

    def swapped(value):
        return lax.ppermute(value, "expert", [(i, i ^ 1) for i in range(n_expert)])

    def across(value, bit):
        return lax.ppermute(value, "dp", [(d, d ^ (1 << bit)) for d in range(n_dp)])

    routes_t, gates_t = routes.T, gate_values.T

    def dispatch(shifts, *moved):
        return pl.pallas_call(
            functools.partial(dispatch_kernel, experts, cap, shifts, len(moved)),
            out_shape=[array(*value.shape) for value in moved]
            + [array(2 * cap, width)] * len(shifts),
            in_specs=[hbm()] * (4 + len(moved)),
            out_specs=[hbm()] * (len(moved) + len(shifts)),
            scratch_shapes=[
                pltpu.VMEM(routes_t.shape, routes_t.dtype),
                pltpu.VMEM(gates_t.shape, gates_t.dtype),
                pltpu.VMEM(tokens.shape, BF),
                pltpu.VMEM(cotangent.shape, BF),
                pltpu.VMEM((len(shifts), 2 * cap, width), BF),
                pltpu.VMEM((len(moved), *moved[0].shape), BF),
                pltpu.SemaphoreType.DMA((4 + 2 * len(moved) + len(shifts),)),
            ],
            compiler_params=params(56),
            cost_estimate=cost(2),
            name="dispatch",
        )(routes_t, gates_t, tokens, cotangent, *moved)

    shifts = list(range(experts))
    far = experts // 2
    groups = [[shift for shift in shifts if shift != far], [far]]
    own, sib = {}, {}
    order = groups[0][1:] + [far, 0]
    up_own, down_own, *sends = dispatch(order, up_weight[0], down_weight[0])
    for shift, send in zip(order, sends):
        own[shift] = shifted(send, shift) if shift else send

    def passed(value, estimate, *after):
        return pl.pallas_call(
            pass_kernel,
            out_shape=array(*value.shape),
            in_specs=[hbm()] * (1 + len(after)),
            out_specs=hbm(),
            input_output_aliases={0: 0},
            compiler_params=params(1),
            cost_estimate=cost(estimate),
            name="after",
        )(value, *after)

    for shift in groups[0]:
        own[shift] = passed(own[shift], 8) if shift else own[shift]
        sib[shift] = swapped(own[shift])

    def gathered(weight, order):
        blocks, layout, held = [weight], [[0]], [0]
        for bit in order:
            blocks.append(
                across(jnp.concatenate(blocks) if len(blocks) > 1 else weight, bit)
            )
            layout.append([peer ^ (1 << bit) for peer in held])
            held = held + layout[-1]
        return blocks, layout

    ups, up_layout = gathered(up_own, orders[0])
    downs, down_layout = gathered(down_own, orders[1])

    def chunk_call(kernel, group, operands, outs, name, estimate):
        count = len(group)
        parts = [array(count * cap, width)] * 2
        return pl.pallas_call(
            functools.partial(kernel[0], cap, count, *kernel[1:]),
            out_shape=parts + outs,
            in_specs=[vmem()] * (2 * count + len(operands)),
            out_specs=[vmem()] * (2 + len(outs)),
            scratch_shapes=[pltpu.VMEM((2 * count * cap, width), BF)] * 2,
            compiler_params=params(20),
            cost_estimate=cost(estimate),
            name=name,
        )(*[own[shift] for shift in group], *[sib[shift] for shift in group], *operands)

    part_own, part_sib, near_grads, *weights = chunk_call(
        (first_kernel, (up_layout, down_layout), n_dp),
        groups[0],
        [*ups, *downs],
        [
            array(n_dp, 2 * half, step),
            array(width, half),
            array(half, width),
            array(width, half),
        ],
        "first",
        10,
    )
    near_grads = lax.psum_scatter(near_grads, "dp", scatter_dimension=0, tiled=True)
    halves = [(part_own, swapped(part_sib))]

    own[far] = passed(own[far], 12, part_own)
    sib[far] = swapped(own[far])

    pairs, ready = {}, {}

    def paired(groups, halves, *after):
        counts = [len(group) for group in groups]
        results = pl.pallas_call(
            functools.partial(pair_kernel, cap, counts),
            out_shape=[array(cap, width)] * sum(counts),
            in_specs=[vmem()] * (2 * len(counts)) + [hbm()] * len(after),
            out_specs=[vmem()] * sum(counts),
            compiler_params=params(16),
            cost_estimate=cost(1),
            name="pair",
        )(*[value for both in halves for value in both], *after)
        for shift, result in zip([shift for group in groups for shift in group], results):
            ready[shift] = result
            pairs[shift] = passed(shifted(result, experts - shift), 20) if shift else result

    paired(groups[:1], halves, own[far])

    named = [ready[groups[0][-1]]]
    part_own, part_sib, *blocks = chunk_call(
        (late_kernel, n_dp, len(named)),
        groups[1],
        [*weights, *named],
        [array(cap, 2 * step + 4 * half)] * n_dp,
        "late",
        4,
    )
    paired(groups[1:], [(part_own, swapped(part_sib))])

    grad_tokens, mark = pl.pallas_call(
        functools.partial(combine_kernel, experts, cap),
        out_shape=[array(rows, width), jax.ShapeDtypeStruct((8, 128), F32)],
        in_specs=[vmem()] * (1 + experts),
        out_specs=[vmem()] * 2,
        compiler_params=params(16),
        cost_estimate=cost(3),
        name="combine",
    )(routes_t, *[pairs[shift] for shift in range(experts)])

    def to_owner(value, peer):
        return lax.ppermute(value, "dp", [(d, d ^ peer) for d in range(n_dp)])

    blocks = [
        to_owner(passed(block, 0.1, ready[far]) if peer & (peer - 1) else block, peer)
        if peer
        else block
        for peer, block in enumerate(blocks)
    ]
    shared = swapped(
        pl.pallas_call(
            share_kernel,
            out_shape=array(n_dp * cap, 2 * step),
            in_specs=[vmem()] * n_dp,
            out_specs=vmem(),
            compiler_params=params(8),
            cost_estimate=cost(1),
            name="share",
        )(*blocks)
    )
    near_grads = near_grads[0]
    specs = [pl.BlockSpec(near_grads.shape, lambda i: (0, 0))]
    specs += [pl.BlockSpec(value.shape, lambda i: (0, 0)) for value in blocks + [shared]]
    specs += [pl.BlockSpec((8, 128), lambda i: (0, 0))]
    grad_up, grad_down = pl.pallas_call(
        functools.partial(last_kernel, n_dp),
        grid=(1,),
        out_shape=[array(1, step, half)] * 2,
        in_specs=specs,
        out_specs=[pl.BlockSpec((1, step, half), lambda i: (0, 0, 0))] * 2,
        scratch_shapes=[
            pltpu.VMEM((2 * n_dp * cap, step), BF),
            pltpu.VMEM((2 * n_dp * cap, half), BF),
        ],
        compiler_params=params(24),
        cost_estimate=cost(4),
        name="grads",
    )(near_grads, *blocks, shared, mark)
    return (grad_tokens, grad_up, grad_down)


def solution(mesh):
    in_specs = (
        P(("dp", "expert"), None),
        P(("dp", "expert"), None),
        P(("dp", "expert"), None),
        P(("dp", "expert"), None),
        P("expert", "dp", None),
        P("expert", "dp", None),
    )
    out_specs = (P(("dp", "expert"), None), P("expert", "dp", None), P("expert", "dp", None))
    return jax.shard_map(
        functools.partial(on_device, mesh.shape["dp"], mesh.shape["expert"]),
        mesh=mesh,
        in_specs=in_specs,
        out_specs=out_specs,
        check_vma=False,
    )
```

time: 306 us -> 146 us (0.48)
  waiting for transfers between devices: 202 us -> 79.6 us
  local copies, waits for them, and re-layouts: 33.3 us -> 7.38 us
  matrix products: 20.8 us -> 0 us
  Pallas kernels: 0 us -> 16.7 us
  other arithmetic: 11 us -> 1.23 us
  starting transfers between devices: 20.4 us -> 24.7 us
    all_to_all x3 -> x0, waiting for transfers between devices: 165 us -> none  [the longest x1 70.8 us: on_device(): lax.all_to_all(by_source, 'expert', split_axis=0, concat_axis=0, tiled=True)]
    ppermute x0 -> x20, waiting for transfers between devices: none -> 79.6 us  [the longest x6 58.1 us: shifted(): return lax.ppermute(value, 'expert', pairs)]
    all_gather x2 -> x0, waiting for transfers between devices: 35.9 us -> none  [the longest x1 35.9 us: on_device(): lax.all_gather(up_weight, 'dp', axis=1, tiled=True)]
    ppermute x0 -> x20, starting transfers between devices: none -> 24.7 us  [the longest x6 9.63 us: shifted(): return lax.ppermute(value, 'expert', pairs)]
    dot_general x5 -> x0, matrix products: 20.8 us -> none  [the longest x1 5.34 us: on_device(): hidden = jnp.dot(rows_x, weight_up, preferred_element_type=jnp.float32)]
    all_to_all x3 -> x0, starting transfers between devices: 20.1 us -> none  [the longest x1 7.23 us: on_device(): lax.all_to_all(doubled_s, 'expert', split_axis=0, concat_axis=0, tiled=True)]
    pallas_call x0 -> x15, Pallas kernels: none -> 16.7 us  [the longest x2 8.47 us: chunk_call(): pl.pallas_call(functools.partial(kernel[0], cap, count, *kernel[1:]), out...]
    gather x4 -> x0, local copies, waits for them, and re-layouts: 10.2 us -> none  [the longest x1 2.59 us: on_device(): send_x = jnp.concatenate([tokens, zero_row])[row_table]]
  transfers between devices with their start and end apart: 6 -> 21, of which waited for: 4 -> 10; matrix products, arithmetic and copies ran while one was open for 10% -> 1% of each run, Pallas kernels for 0% -> 8%
where the time goes in v1:
time: 146 us; the launch traced here: 144 us
  waiting for transfers between devices  79.6 us (55%)
  starting transfers between devices  24.7 us (17%)
  Pallas kernels  16.7 us (11%)
  between operations  14.1 us (10%)
  local copies, waits for them, and re-layouts  7.38 us (5%)
    ppermute x6, waiting for transfers between devices, shifted(): return lax.ppermute(value, 'expert', pairs)  58.1 us
    ppermute x3, waiting for transfers between devices, to_owner(): return lax.ppermute(value, 'dp', [(d, d ^ peer) for d in range(n_dp)])  12.8 us
    ppermute x6, starting transfers between devices, shifted(): return lax.ppermute(value, 'expert', pairs)  9.63 us
    pallas_call x2, Pallas kernels, chunk_call(): pl.pallas_call(functools.partial(kernel[0], cap, count, *kernel[1:]), out...  8.47 us
    ppermute x7, starting transfers between devices, swapped(): return lax.ppermute(value, 'expert', [(i, i ^ 1) for i in range(n_expert)])  7.99 us
    unnamed x24, local copies, waits for them, and re-layouts  7.38 us
    ppermute x4, waiting for transfers between devices, across(): return lax.ppermute(value, 'dp', [(d, d ^ 1 << bit) for d in range(n_dp)])  6.58 us
    ppermute x4, starting transfers between devices, across(): return lax.ppermute(value, 'dp', [(d, d ^ 1 << bit) for d in range(n_dp)])  5.11 us
  transfers between devices with their start and end apart: 21, of which 10 were waited for; matrix products, arithmetic and copies ran while one was open for 1% of the time, Pallas kernels for 8%

profile of v1, /device:TPU:9, one launch (start us, length us, event | category | flops | bytes accessed | tf_op | source)
XLA Modules:
  0.0 143.8 jit_solution(17480418539664665197)
XLA Ops:
  7.2 0.0 reduce-scatter.4.cloned.1.call-start
  7.2 3.8 %dispatch.1 = (bf16[640,384]{1,0:T(8,128)(2,1)}, bf16[640,384]{1,0:T(8,128)(2,1)}, bf16[160,2560]{1,0:T(8,128)(2,1)}, bf16[160,2560]{1,0:T(8,128)(2,1)}, bf16[16...) custom-call(s32[2,128]{1,0:T(2,128)} %bitcast.7, f32[2,128]{1,0:T(2,128)} %bitcast.11, bf16[128,2560]{1,0:T(8,128)(2,1)} %refs_2_.1, ...), custom_call_target="tpu_custom_call" | custom-call | flops 2000000000 | bytes 1048576 | tf_op jit(solution)/shard_map/dispatch/pallas_call | solution.py:263
  11.0 0.0 copy-start.2
  11.1 1.3 collective-permute-start.5
  12.3 1.3 collective-permute-start
  13.6 1.2 collective-permute-start.7
  14.9 0.2 collective-permute-start.1
  15.1 1.8 %collective-permute-start.2 = (bf16[160,2560]{1,0:T(8,128)(2,1)}, bf16[160,2560]{1,0:T(8,128)(2,1)S(1)}, u32[]{:S(2)}, u32[]{:S(2)}) collective-permute-start(bf16[160,2560]{1,0:T(8,128)(2,1)} %get-tuple-element.28.refs_0_), channel_id=1, source_target_pairs={{0,1},{1,0},{2,3},{3,2},{4,5},{5,4},{6,7},{7,6},{8,9},{9,8},{10,11... | collective-permute-start | bytes 2457608 | tf_op jit(solution)/shard_map/ppermute | solution.py:255
  16.8 6.6 %collective-permute-done.5.refs_7_ = bf16[640,384]{1,0:T(8,128)(2,1)S(1)} collective-permute-done((bf16[640,384]{1,0:T(8,128)(2,1)}, bf16[640,384]{1,0:T(8,128)(2,1)S(1)}, u32[]{:S(2)}, u32[]{:S(2)}) %collective-permute-start.5) | collective-permute-done | bytes 491552 | tf_op jit(solution)/shard_map/ppermute | solution.py:258
  23.4 1.1 pad_maximum_fusion
  24.6 1.3 collective-permute-start.6
  25.9 0.0 collective-permute-done.7.refs_10_
  25.9 0.0 copy-done.2
  25.9 0.1 pad_maximum_fusion.1
  26.0 1.3 collective-permute-start.8
  27.3 4.1 %collective-permute-done.refs_0_ = bf16[160,2560]{1,0:T(8,128)(2,1)S(1)} collective-permute-done((bf16[160,2560]{1,0:T(8,128)(2,1)}, bf16[160,2560]{1,0:T(8,128)(2,1)S(1)}, u32[]{:S(2)}, u32[]{:S(2)}) %collective-permute-start) | collective-permute-done | bytes 819232 | tf_op jit(solution)/shard_map/ppermute | solution.py:252
  31.3 3.3 %collective-permute-start.3 = (bf16[160,2560]{1,0:T(8,128)(2,1)S(1)}, bf16[160,2560]{1,0:T(8,128)(2,1)S(1)}, u32[]{:S(2)}, u32[]{:S(2)}) collective-permute-start(bf16[160,2560]{1,0:T(8,128)(2,1)S(1)} %after.7.refs_1_), channel_id=1, source_target_pairs={{0,1},{1,0},{2,3},{3,2},{4,5},{5,4},{6,7},{7,6},{8,9},{9,8},{10,11... | collective-permute-start | bytes 2457608 | tf_op jit(solution)/shard_map/ppermute | solution.py:255
  34.7 16.4 %collective-permute-done.1.refs_0_ = bf16[160,2560]{1,0:T(8,128)(2,1)S(1)} collective-permute-done((bf16[160,2560]{1,0:T(8,128)(2,1)}, bf16[160,2560]{1,0:T(8,128)(2,1)S(1)}, u32[]{:S(2)}, u32[]{:S(2)}) %collective-permute-start.1) | collective-permute-done | bytes 819232 | tf_op jit(solution)/shard_map/ppermute | solution.py:252
  51.1 0.5 collective-permute-start.4
  51.6 0.0 collective-permute-done.2.refs_3_
  51.6 1.6 %collective-permute-start.10 = (bf16[160,2560]{1,0:T(8,128)(2,1)}, bf16[160,2560]{1,0:T(8,128)(2,1)S(1)}, u32[]{:S(2)}, u32[]{:S(2)}) collective-permute-start(bf16[160,2560]{1,0:T(8,128)(2,1)} %get-tuple-element.35), channel_id=1, source_target_pairs={{0,4},{1,5},{2,6},{3,7},{4,0},{5,1},{6,2},{7,3},{8,12},{9,13},{10,... | collective-permute-start | bytes 2457608 | tf_op jit(solution)/shard_map/ppermute | solution.py:252
  53.2 0.0 collective-permute-done.6.refs_8_
  53.2 0.0 collective-permute-done.8.refs_11_
  53.2 0.0 collective-permute-done.3.refs_4_
  53.2 0.4 collective-permute-done.4.refs_5_
  53.6 0.0 copy-done.1
  53.6 0.0 copy-done.4
  53.6 6.9 %first.1 = (bf16[240,2560]{1,0:T(8,128)(2,1)S(1)}, bf16[240,2560]{1,0:T(8,128)(2,1)S(1)}, bf16[4,768,640]{2,1,0:T(8,128)(2,1)S(1)}, bf16[2560,384]{1,0:T(8,128)(...) custom-call(bf16[160,2560]{1,0:T(8,128)(2,1)S(1)} %copy-done.4, ...), custom_call_target="tpu_custom_call" | custom-call | flops 10000000000 | bytes 1048576 | tf_op jit(solution)/shard_map/first/pallas_call | solution.py:324
  60.5 0.0 copy-start
  60.5 1.9 %copy-done = bf16[4,768,640]{2,1,0:T(8,128)(2,1)} copy-done((bf16[4,768,640]{2,1,0:T(8,128)(2,1)}, bf16[4,768,640]{2,1,0:T(8,128)(2,1)S(1)}, u32[]{:S(2)}) %copy-start) | copy-done | bytes 3932184
  62.3 1.3 copy-done.6
  63.6 1.3 copy-done.8
  64.9 1.3 copy-done.10
  66.3 0.0 reduce-scatter.4.cloned.1.call-update
  66.3 0.4 collective-permute-start.9
  66.7 22.2 %collective-permute-done.10.refs_0_ = bf16[160,2560]{1,0:T(8,128)(2,1)S(1)} collective-permute-done((bf16[160,2560]{1,0:T(8,128)(2,1)}, bf16[160,2560]{1,0:T(8,128)(2,1)S(1)}, u32[]{:S(2)}, u32[]{:S(2)}) %collective-permute-start.10) | collective-permute-done | bytes 819232 | tf_op jit(solution)/shard_map/ppermute | solution.py:252
  88.9 0.5 collective-permute-start.12
  89.4 0.0 collective-permute-done.9.refs_1_
  89.4 0.3 pair.2
  89.7 1.7 %collective-permute-done.12.refs_1_ = bf16[160,2560]{1,0:T(8,128)(2,1)S(1)} collective-permute-done((bf16[160,2560]{1,0:T(8,128)(2,1)S(1)}, bf16[160,2560]{1,0:T(8,128)(2,1)S(1)}, u32[]{:S(2)}, u32[]{:S(2)}) %collective-permute-start.12) | collective-permute-done | bytes 819232 | tf_op jit(solution)/shard_map/ppermute | solution.py:255
  91.4 0.4 copy-done.7
  91.7 1.6 %late.1 = (bf16[80,2560]{1,0:T(8,128)(2,1)S(1)}, bf16[80,2560]{1,0:T(8,128)(2,1)S(1)}, bf16[80,2816]{1,0:T(8,128)(2,1)S(1)}, bf16[80,2816]{1,0:T(8,128)(2,1)S(1)...) custom-call(bf16[160,2560]{1,0:T(8,128)(2,1)S(1)} %after.9.refs_2_.refs_0_, ...), custom_call_target="tpu_custom_call" | custom-call | flops 4000000000 | bytes 1048576 | tf_op jit(solution)/shard_map/late/pallas_call | solution.py:324
  93.3 0.5 collective-permute-start.13
  93.8 2.7 %collective-permute-start.11 = (bf16[80,2560]{1,0:T(8,128)(2,1)S(1)}, bf16[80,2560]{1,0:T(8,128)(2,1)S(1)}, u32[]{:S(2)}, u32[]{:S(2)}) collective-permute-start(bf16[80,2560]{1,0:T(8,128)(2,1)S(1)} %get-tuple-element.37), channel_id=1, source_target_pairs={{0,6},{1,7},{2,0},{3,1},{4,2},{5,3},{6,4},{7,5},{8,14},{9,15},{10,... | collective-permute-start | bytes 1228808 | tf_op jit(solution)/shard_map/ppermute | solution.py:252
  96.6 0.0 collective-permute-start.15
  96.6 0.2 collective-permute-start.16
  96.8 1.0 collective-permute-start.17
  97.8 0.0 collective-permute-done.13.refs_1_
  97.8 0.1 pair.3.refs_1_
  97.9 3.9 %collective-permute-start.14 = (bf16[80,2560]{1,0:T(8,128)(2,1)S(1)}, bf16[80,2560]{1,0:T(8,128)(2,1)S(1)}, u32[]{:S(2)}, u32[]{:S(2)}) collective-permute-start(bf16[80,2560]{1,0:T(8,128)(2,1)S(1)} %pair.3.refs_1_), channel_id=1, source_target_pairs={{0,4},{1,5},{2,6},{3,7},{4,0},{5,1},{6,2},{7,3},{8,12},{9,13},{10,... | collective-permute-start | bytes 1228808 | tf_op jit(solution)/shard_map/ppermute | solution.py:252
  101.7 13.9 %collective-permute-done.11.refs_0_ = bf16[80,2560]{1,0:T(8,128)(2,1)S(1)} collective-permute-done((bf16[80,2560]{1,0:T(8,128)(2,1)S(1)}, bf16[80,2560]{1,0:T(8,128)(2,1)S(1)}, u32[]{:S(2)}, u32[]{:S(2)}) %collective-permute-start.11) | collective-permute-done | bytes 409632 | tf_op jit(solution)/shard_map/ppermute | solution.py:252
  115.6 0.7 collective-permute-start.18
  116.4 0.1 collective-permute-done.15.refs_0_
  116.5 0.0 collective-permute-done.16.refs_1_.refs_2_
  116.5 0.0 collective-permute-done.17.refs_2_.refs_3_
  116.5 12.8 %collective-permute-done.18.refs_3_.refs_4_ = bf16[80,2816]{1,0:T(8,128)(2,1)S(1)} collective-permute-done((bf16[80,2816]{1,0:T(8,128)(2,1)S(1)}, bf16[80,2816]{1,0:T(8,128)(2,1)S(1)}, u32[]{:S(2)}, u32[]{:S(2)}) %collective-permute-start.18) | collective-permute-done | bytes 450592 | tf_op jit(solution)/shard_map/ppermute | solution.py:395
  129.3 0.1 share.1
  129.4 0.0 copy-start.5
  129.4 0.9 collective-permute-start.19
  130.3 1.5 %collective-permute-done.14.refs_0_ = bf16[80,2560]{1,0:T(8,128)(2,1)S(1)} collective-permute-done((bf16[80,2560]{1,0:T(8,128)(2,1)S(1)}, bf16[80,2560]{1,0:T(8,128)(2,1)S(1)}, u32[]{:S(2)}, u32[]{:S(2)}) %collective-permute-start.14) | collective-permute-done | bytes 409632 | tf_op jit(solution)/shard_map/ppermute | solution.py:252
  131.7 1.9 %combine.1 = (bf16[128,2560]{1,0:T(8,128)(2,1)}, f32[8,128]{1,0:T(8,128)S(1)}) custom-call(s32[2,128]{1,0:T(2,128)S(1)} %bitcast.8, bf16[80,2560]{1,0:T(8,128)(2,1)S(1)} %get-tuple-element.36.rest_0_, bf16[80,2560]{1,0:T(8,128)(2,1)S(1)} %after.10.rest_1_, bf16[80,2560]{1,0:T(8,128)(2,1)S(1)} %after.11.rest_2_, bf16[80,2560]{1,0:T(8,128)(2,1)S(1)} %after.12.rest_3_), custom_call_target="tpu_custom_call" | custom-call | flops 3000000000 | bytes 1048576 | tf_op jit(solution)/shard_map/combine/pallas_call | solution.py:384
  133.7 0.0 collective-permute-done.19.refs_5_
  133.7 1.2 copy-done.3
  134.9 2.1 %grads.1 = (bf16[1,640,384]{2,1,0:T(8,128)(2,1)}, bf16[1,640,384]{2,1,0:T(8,128)(2,1)}) custom-call(bf16[768,640]{1,0:T(8,128)(2,1)S(1)} %bitcast.6, bf16[80,2816]{1,0:T(8,128)(2,1)S(1)} %get-tuple-element.46.refs_0_.refs_1_, bf16[80,2816]{1,0:T(8,128)(2,1)S(1)} %collective-permute-done.16.refs_1_.refs_2_, ...), custom_call_target="tpu_custom_call" | custom-call | flops 4000000000 | bytes 1048576 | tf_op jit(solution)/shard_map/grads/pallas_call | solution.py:418
  (20 shorter events, 0.0 us)
Async XLA Ops:
  7.2 126.5 %reduce-scatter.4.cloned.1.call-start = ((), (), s32[]{:S(2)}) async-start(), calls=%async_computation.1 | async-start | bytes 4915200
  11.0 14.8 %copy-start.2 = (bf16[640,384]{1,0:T(8,128)(2,1)S(1)}, bf16[640,384]{1,0:T(8,128)(2,1)}, u32[]{:S(2)}) copy-start(bf16[640,384]{1,0:T(8,128)(2,1)} %get-tuple-element.32.refs_9_) | copy-start | bytes 1474564
  11.1 12.4 %collective-permute-start.5 = (bf16[640,384]{1,0:T(8,128)(2,1)}, bf16[640,384]{1,0:T(8,128)(2,1)S(1)}, u32[]{:S(2)}, u32[]{:S(2)}) collective-permute-start(bf16[640,384]{1,0:T(8,128)(2,1)} %get-tuple-element.31.refs_6_), channel_id=1, source_target_pairs={{0,8},{8,0},{16,24},{24,16},{1,9},{9,1},{17,25},{25,17},{2,10},{10... | collective-permute-start | bytes 1474568 | tf_op jit(solution)/shard_map/ppermute | solution.py:258
  12.3 19.0 %collective-permute-start = (bf16[160,2560]{1,0:T(8,128)(2,1)}, bf16[160,2560]{1,0:T(8,128)(2,1)S(1)}, u32[]{:S(2)}, u32[]{:S(2)}) collective-permute-start(bf16[160,2560]{1,0:T(8,128)(2,1)} %get-tuple-element.29), channel_id=1, source_target_pairs={{0,2},{1,3},{2,4},{3,5},{4,6},{5,7},{6,0},{7,1},{8,10},{9,11},{10,... | collective-permute-start | bytes 2457608 | tf_op jit(solution)/shard_map/ppermute | solution.py:252
  13.6 12.2 %collective-permute-start.7 = (bf16[640,384]{1,0:T(8,128)(2,1)}, bf16[640,384]{1,0:T(8,128)(2,1)S(1)}, u32[]{:S(2)}, u32[]{:S(2)}) collective-permute-start(bf16[640,384]{1,0:T(8,128)(2,1)} %get-tuple-element.32.refs_9_), channel_id=1, source_target_pairs={{0,16},{8,24},{16,0},{24,8},{1,17},{9,25},{17,1},{25,9},{2,18},{10... | collective-permute-start | bytes 1474568 | tf_op jit(solution)/shard_map/ppermute | solution.py:258
  14.9 36.2 %collective-permute-start.1 = (bf16[160,2560]{1,0:T(8,128)(2,1)}, bf16[160,2560]{1,0:T(8,128)(2,1)S(1)}, u32[]{:S(2)}, u32[]{:S(2)}) collective-permute-start(bf16[160,2560]{1,0:T(8,128)(2,1)} %get-tuple-element.30), channel_id=1, source_target_pairs={{0,6},{1,7},{2,0},{3,1},{4,2},{5,3},{6,4},{7,5},{8,14},{9,15},{10,... | collective-permute-start | bytes 2457608 | tf_op jit(solution)/shard_map/ppermute | solution.py:252
  15.1 36.6 %collective-permute-start.2 = (bf16[160,2560]{1,0:T(8,128)(2,1)}, bf16[160,2560]{1,0:T(8,128)(2,1)S(1)}, u32[]{:S(2)}, u32[]{:S(2)}) collective-permute-start(bf16[160,2560]{1,0:T(8,128)(2,1)} %get-tuple-element.28.refs_0_), channel_id=1, source_target_pairs={{0,1},{1,0},{2,3},{3,2},{4,5},{5,4},{6,7},{7,6},{8,9},{9,8},{10,11... | collective-permute-start | bytes 2457608 | tf_op jit(solution)/shard_map/ppermute | solution.py:255
  24.6 28.6 %collective-permute-start.6 = (bf16[1280,384]{1,0:T(8,128)(2,1)S(1)}, bf16[1280,384]{1,0:T(8,128)(2,1)S(1)}, u32[]{:S(2)}, u32[]{:S(2)}) collective-permute-start(bf16[1280,384]{1,0:T(8,128)(2,1)S(1)} %pad_maximum_fusion), channel_id=1, source_target_pairs={{0,16},{8,24},{16,0},{24,8},{1,17},{9,25},{17,1},{25,9},{2,18},{10... | collective-permute-start | bytes 2949128 | tf_op jit(solution)/shard_map/ppermute | solution.py:258
  26.0 27.2 %collective-permute-start.8 = (bf16[1280,384]{1,0:T(8,128)(2,1)S(1)}, bf16[1280,384]{1,0:T(8,128)(2,1)S(1)}, u32[]{:S(2)}, u32[]{:S(2)}) collective-permute-start(bf16[1280,384]{1,0:T(8,128)(2,1)S(1)} %pad_maximum_fusion.1), channel_id=1, source_target_pairs={{0,8},{8,0},{16,24},{24,16},{1,9},{9,1},{17,25},{25,17},{2,10},{10... | collective-permute-start | bytes 2949128 | tf_op jit(solution)/shard_map/ppermute | solution.py:258
  31.3 22.2 %copy-start.1 = (bf16[640,384]{1,0:T(8,128)(2,1)S(1)}, bf16[640,384]{1,0:T(8,128)(2,1)}, u32[]{:S(2)}) copy-start(bf16[640,384]{1,0:T(8,128)(2,1)} %get-tuple-element.31.refs_6_) | copy-start | bytes 1474564
  31.3 22.2 %copy-start.4 = (bf16[160,2560]{1,0:T(8,128)(2,1)S(1)}, bf16[160,2560]{1,0:T(8,128)(2,1)}, u32[]{:S(2)}) copy-start(bf16[160,2560]{1,0:T(8,128)(2,1)} %get-tuple-element.28.refs_0_) | copy-start | bytes 2457604
  31.3 21.8 %collective-permute-start.3 = (bf16[160,2560]{1,0:T(8,128)(2,1)S(1)}, bf16[160,2560]{1,0:T(8,128)(2,1)S(1)}, u32[]{:S(2)}, u32[]{:S(2)}) collective-permute-start(bf16[160,2560]{1,0:T(8,128)(2,1)S(1)} %after.7.refs_1_), channel_id=1, source_target_pairs={{0,1},{1,0},{2,3},{3,2},{4,5},{5,4},{6,7},{7,6},{8,9},{9,8},{10,11... | collective-permute-start | bytes 2457608 | tf_op jit(solution)/shard_map/ppermute | solution.py:255
  51.1 2.5 %collective-permute-start.4 = (bf16[160,2560]{1,0:T(8,128)(2,1)S(1)}, bf16[160,2560]{1,0:T(8,128)(2,1)S(1)}, u32[]{:S(2)}, u32[]{:S(2)}) collective-permute-start(bf16[160,2560]{1,0:T(8,128)(2,1)S(1)} %after.8.refs_2_), channel_id=1, source_target_pairs={{0,1},{1,0},{2,3},{3,2},{4,5},{5,4},{6,7},{7,6},{8,9},{9,8},{10,11... | collective-permute-start | bytes 2457608 | tf_op jit(solution)/shard_map/ppermute | solution.py:255
  51.6 37.3 %collective-permute-start.10 = (bf16[160,2560]{1,0:T(8,128)(2,1)}, bf16[160,2560]{1,0:T(8,128)(2,1)S(1)}, u32[]{:S(2)}, u32[]{:S(2)}) collective-permute-start(bf16[160,2560]{1,0:T(8,128)(2,1)} %get-tuple-element.35), channel_id=1, source_target_pairs={{0,4},{1,5},{2,6},{3,7},{4,0},{5,1},{6,2},{7,3},{8,12},{9,13},{10,... | collective-permute-start | bytes 2457608 | tf_op jit(solution)/shard_map/ppermute | solution.py:252
  60.5 1.9 %copy-start = (bf16[4,768,640]{2,1,0:T(8,128)(2,1)}, bf16[4,768,640]{2,1,0:T(8,128)(2,1)S(1)}, u32[]{:S(2)}) copy-start(bf16[4,768,640]{2,1,0:T(8,128)(2,1)S(1)} %get-tuple-element.45) | copy-start | bytes 11796484
  62.3 1.3 copy-start.6
  63.6 1.3 copy-start.8
  64.9 1.3 copy-start.10
  66.3 23.1 %collective-permute-start.9 = (bf16[240,2560]{1,0:T(8,128)(2,1)S(1)}, bf16[240,2560]{1,0:T(8,128)(2,1)S(1)}, u32[]{:S(2)}, u32[]{:S(2)}) collective-permute-start(bf16[240,2560]{1,0:T(8,128)(2,1)S(1)} %get-tuple-element.34), channel_id=1, source_target_pairs={{0,1},{1,0},{2,3},{3,2},{4,5},{5,4},{6,7},{7,6},{8,9},{9,8},{10,11... | collective-permute-start | bytes 3686408 | tf_op jit(solution)/shard_map/ppermute | solution.py:255
  88.9 2.5 %copy-start.9 = (bf16[384,2560]{1,0:T(8,128)(2,1)S(1)}, bf16[384,2560]{1,0:T(8,128)(2,1)}, u32[]{:S(2)}) copy-start(bf16[384,2560]{1,0:T(8,128)(2,1)} %copy-done.8) | copy-start | bytes 5898244
  88.9 2.5 %copy-start.11 = (bf16[2560,384]{1,0:T(8,128)(2,1)S(1)}, bf16[2560,384]{1,0:T(8,128)(2,1)}, u32[]{:S(2)}) copy-start(bf16[2560,384]{1,0:T(8,128)(2,1)} %copy-done.10) | copy-start | bytes 5898244
  88.9 2.8 %copy-start.7 = (bf16[2560,384]{1,0:T(8,128)(2,1)S(1)}, bf16[2560,384]{1,0:T(8,128)(2,1)}, u32[]{:S(2)}) copy-start(bf16[2560,384]{1,0:T(8,128)(2,1)} %copy-done.6) | copy-start | bytes 5898244
  88.9 2.4 %collective-permute-start.12 = (bf16[160,2560]{1,0:T(8,128)(2,1)S(1)}, bf16[160,2560]{1,0:T(8,128)(2,1)S(1)}, u32[]{:S(2)}, u32[]{:S(2)}) collective-permute-start(bf16[160,2560]{1,0:T(8,128)(2,1)S(1)} %after.9.refs_2_.refs_0_), channel_id=1, source_target_pairs={{0,1},{1,0},{2,3},{3,2},{4,5},{5,4},{6,7},{7,6},{8,9},{9,8},{10,11... | collective-permute-start | bytes 2457608 | tf_op jit(solution)/shard_map/ppermute | solution.py:255
  93.3 4.5 %collective-permute-start.13 = (bf16[80,2560]{1,0:T(8,128)(2,1)S(1)}, bf16[80,2560]{1,0:T(8,128)(2,1)S(1)}, u32[]{:S(2)}, u32[]{:S(2)}) collective-permute-start(bf16[80,2560]{1,0:T(8,128)(2,1)S(1)} %get-tuple-element.43), channel_id=1, source_target_pairs={{0,1},{1,0},{2,3},{3,2},{4,5},{5,4},{6,7},{7,6},{8,9},{9,8},{10,11... | collective-permute-start | bytes 1228808 | tf_op jit(solution)/shard_map/ppermute | solution.py:255
  93.8 21.8 %collective-permute-start.11 = (bf16[80,2560]{1,0:T(8,128)(2,1)S(1)}, bf16[80,2560]{1,0:T(8,128)(2,1)S(1)}, u32[]{:S(2)}, u32[]{:S(2)}) collective-permute-start(bf16[80,2560]{1,0:T(8,128)(2,1)S(1)} %get-tuple-element.37), channel_id=1, source_target_pairs={{0,6},{1,7},{2,0},{3,1},{4,2},{5,3},{6,4},{7,5},{8,14},{9,15},{10,... | collective-permute-start | bytes 1228808 | tf_op jit(solution)/shard_map/ppermute | solution.py:252
  96.6 19.9 %collective-permute-start.15 = (bf16[80,2560]{1,0:T(8,128)(2,1)S(1)}, bf16[80,2560]{1,0:T(8,128)(2,1)S(1)}, u32[]{:S(2)}, u32[]{:S(2)}) collective-permute-start(bf16[80,2560]{1,0:T(8,128)(2,1)S(1)} %get-tuple-element.41.refs_5_), channel_id=1, source_target_pairs={{0,2},{1,3},{2,4},{3,5},{4,6},{5,7},{6,0},{7,1},{8,10},{9,11},{10,... | collective-permute-start | bytes 1228808 | tf_op jit(solution)/shard_map/ppermute | solution.py:252
  96.6 19.9 %collective-permute-start.16 = (bf16[80,2816]{1,0:T(8,128)(2,1)S(1)}, bf16[80,2816]{1,0:T(8,128)(2,1)S(1)}, u32[]{:S(2)}, u32[]{:S(2)}) collective-permute-start(bf16[80,2816]{1,0:T(8,128)(2,1)S(1)} %get-tuple-element.47), channel_id=1, source_target_pairs={{0,8},{8,0},{16,24},{24,16},{1,9},{9,1},{17,25},{25,17},{2,10},{10... | collective-permute-start | bytes 1351688 | tf_op jit(solution)/shard_map/ppermute | solution.py:395
  96.8 19.7 %collective-permute-start.17 = (bf16[80,2816]{1,0:T(8,128)(2,1)S(1)}, bf16[80,2816]{1,0:T(8,128)(2,1)S(1)}, u32[]{:S(2)}, u32[]{:S(2)}) collective-permute-start(bf16[80,2816]{1,0:T(8,128)(2,1)S(1)} %get-tuple-element.48), channel_id=1, source_target_pairs={{0,16},{8,24},{16,0},{24,8},{1,17},{9,25},{17,1},{25,9},{2,18},{10... | collective-permute-start | bytes 1351688 | tf_op jit(solution)/shard_map/ppermute | solution.py:395
  97.9 33.9 %collective-permute-start.14 = (bf16[80,2560]{1,0:T(8,128)(2,1)S(1)}, bf16[80,2560]{1,0:T(8,128)(2,1)S(1)}, u32[]{:S(2)}, u32[]{:S(2)}) collective-permute-start(bf16[80,2560]{1,0:T(8,128)(2,1)S(1)} %pair.3.refs_1_), channel_id=1, source_target_pairs={{0,4},{1,5},{2,6},{3,7},{4,0},{5,1},{6,2},{7,3},{8,12},{9,13},{10,... | collective-permute-start | bytes 1228808 | tf_op jit(solution)/shard_map/ppermute | solution.py:252
  115.6 13.7 %collective-permute-start.18 = (bf16[80,2816]{1,0:T(8,128)(2,1)S(1)}, bf16[80,2816]{1,0:T(8,128)(2,1)S(1)}, u32[]{:S(2)}, u32[]{:S(2)}) collective-permute-start(bf16[80,2816]{1,0:T(8,128)(2,1)S(1)} %after.13), channel_id=1, source_target_pairs={{0,24},{8,16},{16,8},{24,0},{1,25},{9,17},{17,9},{25,1},{2,26},{10... | collective-permute-start | bytes 1351688 | tf_op jit(solution)/shard_map/ppermute | solution.py:395
  129.4 2.4 %copy-start.5 = (s32[128,2]{0,1:T(2,128)S(1)}, s32[128,2]{0,1:T(2,128)}, u32[]{:S(2)}) copy-start(s32[128,2]{0,1:T(2,128)} %param.8) | copy-start | bytes 3076
  129.4 4.3 %collective-permute-start.19 = (bf16[320,1280]{1,0:T(8,128)(2,1)S(1)}, bf16[320,1280]{1,0:T(8,128)(2,1)S(1)}, u32[]{:S(2)}, u32[]{:S(2)}) collective-permute-start(bf16[320,1280]{1,0:T(8,128)(2,1)S(1)} %share.1), channel_id=1, source_target_pairs={{0,1},{1,0},{2,3},{3,2},{4,5},{5,4},{6,7},{7,6},{8,9},{9,8},{10,11... | collective-permute-start | bytes 2457608 | tf_op jit(solution)/shard_map/ppermute | solution.py:255
  133.7 1.2 copy-start.3
Sparse Core Ops, SparseCore 0:
  66.4 54.8 reduce-scatter.3

commit v2 on v1

--- a/solution.py
+++ b/solution.py
@@ -55,6 +55,36 @@
     slot = lax.broadcasted_iota(jnp.int32, (cap, first.shape[1]), 0)
     here = slot == own.astype(jnp.int32)
     return here & (first == chosen), here & (second == chosen)
+
+
+def slot_pick(plan, gates, chosen, cap):
+    mask0, mask1 = slot_masks(plan, chosen, cap)
+    gate = jnp.sum(
+        jnp.where(mask0, gates[0:1, :], 0.0) + jnp.where(mask1, gates[1:2, :], 0.0),
+        axis=1,
+        keepdims=True,
+    )
+    return jnp.where(mask0 | mask1, 1.0, 0.0).astype(BF), gate
+
+
+def relay_x_kernel(cap, plan_ref, tok_ref, cot_ref, keep_ref, on_ref, cot_out):
+    chip = lax.axis_index("expert") // 2
+    values = plan_ref[...]
+    plan = slot_plan(values[0:2, :].astype(jnp.int32))
+    for chosen, out in ((chip, keep_ref), (chip ^ 1, on_ref)):
+        pick, _ = slot_pick(plan, values[2:4, :], chosen, cap)
+        out[...] = contract(pick, tok_ref[...], 1, 0).astype(BF)
+    cot_out[...] = cot_ref[...]
+
+
+def relay_s_kernel(cap, plan_ref, cot_ref, kept_ref, named_ref, keep_ref, on_ref):
+    chip = lax.axis_index("expert") // 2
+    values = plan_ref[...]
+    plan = slot_plan(values[0:2, :].astype(jnp.int32))
+    keep_ref[:cap, :] = kept_ref[...]
+    for chosen, out, start in ((chip, keep_ref, cap), (chip ^ 1, on_ref, 0)):
+        pick, gate = slot_pick(plan, values[2:4, :], chosen, cap)
+        out[start : start + cap, :] = (gate * contract(pick, cot_ref[...], 1, 0)).astype(BF)
 
 
 def dispatch_kernel(experts, cap, shifts, moved, *refs):
@@ -79,13 +109,7 @@
     for one in copies[2:4]:
         one.wait()
     for index, shift in enumerate(shifts):
-        mask0, mask1 = slot_masks(plan, lax.rem(chip + shift, experts), cap)
-        gate = jnp.sum(
-            jnp.where(mask0, gates[0:1, :], 0.0) + jnp.where(mask1, gates[1:2, :], 0.0),
-            axis=1,
-            keepdims=True,
-        )
-        pick = jnp.where(mask0 | mask1, 1.0, 0.0).astype(BF)
+        pick, gate = slot_pick(plan, gates, chip ^ shift, cap)
         made[index, :cap, :] = contract(pick, tok_ref[...], 1, 0).astype(BF)
         made[index, cap:, :] = (gate * contract(pick, cot_ref[...], 1, 0)).astype(BF)
         copy(made.at[index], outs[index])
@@ -103,7 +127,7 @@
     plan = slot_plan(routes_ref[...])
     picks = []
     for shift in range(experts):
-        mask0, mask1 = slot_masks(plan, lax.rem(chip + shift, experts), cap)
+        mask0, mask1 = slot_masks(plan, chip ^ shift, cap)
         picks.append(jnp.where(mask0 | mask1, 1.0, 0.0).astype(BF).T)
     width = out_ref.shape[1]
     tile = 640
@@ -145,12 +169,13 @@
         part_sib[:, cols] = part[half_rows:]
 
 
-def first_kernel(cap, count, layout, n_dp, *refs):
+def first_kernel(cap, count, layout, *refs):
     owns, sibs, refs = refs[:count], refs[count : 2 * count], refs[2 * count :]
     n_up, n_down = len(layout[0]), len(layout[1])
     ups, downs = refs[:n_up], refs[n_up : n_up + n_down]
-    part_own, part_sib, grads, up, up_turned, down, rows_x, rows_s = refs[n_up + n_down :]
-    step, half = ups[0].shape
+    refs = refs[n_up + n_down :]
+    part_own, part_sib, sum_up, sum_down, up, up_turned, down, rows_x, rows_s = refs
+    step = ups[0].shape[0]
     me = lax.axis_index("dp")
     for full, lay, blocks in ((up, layout[0], ups), (down, layout[1], downs)):
         for peers, block in zip(lay, blocks):
@@ -160,35 +185,40 @@
     up_turned[...] = up[...].T
     chunk_rows(cap, owns, sibs, rows_x, rows_s)
     active, back_hidden = expert_work(rows_x, rows_s, up, down)
-    for base, units, rows in ((0, back_hidden, rows_x), (half, active, rows_s)):
+    partial_rows(back_hidden, up_turned, part_own, part_sib)
+    for units, rows, total in ((active, rows_s, sum_down), (back_hidden, rows_x, sum_up)):
         turned = units.T
-        for owner in range(n_dp):
-            cols = slice(owner * step, (owner + 1) * step)
-            grads[owner, base : base + half, :] = contract(turned, rows[:, cols], 1, 0).astype(BF)
-    partial_rows(back_hidden, up_turned, part_own, part_sib)
-
-
-def late_kernel(cap, count, n_dp, named, *refs):
-    owns, sibs, refs = refs[:count], refs[count : 2 * count], refs[2 * count :]
-    up, up_turned, down = refs[:3]
-    refs = refs[3 + named :]
-    part_own, part_sib, outs = refs[0], refs[1], refs[2 : 2 + n_dp]
-    rows_x, rows_s = refs[2 + n_dp :]
-    half = up_turned.shape[0]
-    step = (outs[0].shape[1] - 4 * half) // 2
-    rows = outs[0].shape[0]
+        for cols in tiles(total.shape[1]):
+            total[:, cols] = contract(turned, rows[:, cols], 1, 0)
+
+
+def tail_kernel(cap, count, order_up, order_down, *refs):
+    x_own, s_own, x_sib, s_sib = refs[:4]
+    refs = refs[4:]
+    up, up_turned, down, up_in, down_in = refs[:5]
+    refs = refs[6:]
+    part_own, part_sib = refs[:2]
+    cut = len(order_up) // 2
+    up_outs, down_outs = refs[2 : 3 + cut], refs[3 + cut : 4 + 2 * cut]
+    rows_x, rows_s = refs[4 + 2 * cut :]
+    half, step = up_outs[1].shape
     me = lax.axis_index("dp")
-    chunk_rows(cap, owns, sibs, rows_x, rows_s)
+    for rows, own, sib in ((rows_x, x_own, x_sib), (rows_s, s_own, s_sib)):
+        rows[:cap, :] = own[...]
+        rows[cap:, :] = sib[...]
     active, back_hidden = expert_work(rows_x, rows_s, up, down)
-    for peer, out in enumerate(outs):
-        cols = pl.ds(pl.multiple_of((me ^ peer) * step, 128), step)
-        out[:, :step] = rows_x[:rows, cols]
-        out[:, step : 2 * step] = rows_s[:rows, cols]
-        first = 2 * step
-        for units in (back_hidden, active):
-            for place in (slice(0, rows), slice(rows, 2 * rows)):
-                out[:, first : first + half] = units[place]
-                first += half
+    for units, rows, before, order, outs in (
+        (active, rows_s, down_in, order_down, down_outs),
+        (back_hidden, rows_x, up_in, order_up, up_outs),
+    ):
+        turned = units.T
+        for place, peer in enumerate(order):
+            cols = pl.ds(pl.multiple_of((me ^ peer) * step, 128), step)
+            block = (before[:, cols] + contract(turned, rows[:, cols], 1, 0)).astype(BF)
+            if place < cut:
+                outs[0][place * half : (place + 1) * half, :] = block
+            else:
+                outs[1 + place - cut][...] = block
     partial_rows(back_hidden, up_turned, part_own, part_sib)
 
 
@@ -209,31 +239,11 @@
     pass
 
 
-def share_kernel(*refs):
-    blocks, out = refs[:-1], refs[-1]
-    rows = blocks[0].shape[0]
-    for index, block in enumerate(blocks):
-        out[index * rows : (index + 1) * rows, :] = block[:, : out.shape[1]]
-
-
-def last_kernel(n_dp, *refs):
-    near, blocks, shared = refs[0], refs[1 : 1 + n_dp], refs[1 + n_dp]
-    out_up, out_down, rows, units = refs[-4:]
-    step, half = rows.shape[1], units.shape[1]
-    count = blocks[0].shape[0]
-    for base, out in ((0, out_up), (1, out_down)):
-        cols = slice(base * step, (base + 1) * step)
-        first = 2 * step + 2 * base * half
-        for index, block in enumerate(blocks):
-            place = slice(2 * index * count, (2 * index + 1) * count)
-            rows[place, :] = block[:, cols]
-            units[place, :] = block[:, first : first + half]
-            place = slice((2 * index + 1) * count, (2 * index + 2) * count)
-            rows[place, :] = shared[index * count : (index + 1) * count, cols]
-            units[place, :] = block[:, first + half : first + 2 * half]
-        total = contract(units[...].T, rows[...], 1, 0)
-        total = total + near[base * half : (base + 1) * half, :].astype(F32)
-        out[0] = total.T.astype(BF)
+def last_kernel(count, *refs):
+    total = refs[0][...].astype(F32)
+    for term in refs[1:count]:
+        total = total + term[...].astype(F32)
+    refs[-1][0] = total.T.astype(BF)
 
 
 def on_device(n_dp, n_expert, tokens, cotangent, routes, gate_values, up_weight, down_weight):
@@ -246,9 +256,7 @@
     orders = (list(range(bits)), list(range(bits))[::-1])
 
     def shifted(value, shift):
-        pairs = [
-            (2 * z + c, 2 * ((z + shift) % experts) + c) for z in range(experts) for c in range(2)
-        ]
+        pairs = [(2 * z + c, 2 * (z ^ shift) + c) for z in range(experts) for c in range(2)]
         return lax.ppermute(value, "expert", pairs)
 
     def swapped(value):
@@ -280,15 +288,6 @@
             name="dispatch",
         )(routes_t, gates_t, tokens, cotangent, *moved)
 
-    shifts = list(range(experts))
-    far = experts // 2
-    groups = [[shift for shift in shifts if shift != far], [far]]
-    own, sib = {}, {}
-    order = groups[0][1:] + [far, 0]
-    up_own, down_own, *sends = dispatch(order, up_weight[0], down_weight[0])
-    for shift, send in zip(order, sends):
-        own[shift] = shifted(send, shift) if shift else send
-
     def passed(value, estimate, *after):
         return pl.pallas_call(
             pass_kernel,
@@ -301,8 +300,41 @@
             name="after",
         )(value, *after)
 
+    shifts = list(range(experts))
+    groups = [shifts[:-1], shifts[-1:]]
+    own, sib = {}, {}
+    relayed = experts == 4
+    order = [1, 0] if relayed else shifts[1:] + [0]
+    up_own, down_own, *sends = dispatch(order, up_weight[0], down_weight[0])
+    for shift, send in zip(order, sends):
+        own[shift] = shifted(send, shift) if shift else send
+    if relayed:
+        plan = shifted(jnp.concatenate([routes_t.astype(F32), gates_t]), 2)
+        landed = shifted(tokens, 2)
+        kept, on_x, cot = pl.pallas_call(
+            functools.partial(relay_x_kernel, cap),
+            out_shape=[array(cap, width)] * 2 + [array(rows, width)],
+            in_specs=[vmem()] * 3,
+            out_specs=[vmem()] * 3,
+            compiler_params=params(12),
+            cost_estimate=cost(1),
+            name="relay_x",
+        )(plan, landed, cotangent)
+        far_x = shifted(on_x, 1)
+        landed = shifted(cot, 2)
+        own[2], on_s = pl.pallas_call(
+            functools.partial(relay_s_kernel, cap),
+            out_shape=[array(2 * cap, width), array(cap, width)],
+            in_specs=[vmem()] * 4,
+            out_specs=[vmem()] * 2,
+            compiler_params=params(12),
+            cost_estimate=cost(1),
+            name="relay_s",
+        )(plan, landed, kept, far_x)
+        far_s = shifted(on_s, 1)
+    else:
+        far_x, far_s = own[experts - 1][:cap], own[experts - 1][cap:]
     for shift in groups[0]:
-        own[shift] = passed(own[shift], 8) if shift else own[shift]
         sib[shift] = swapped(own[shift])
 
     def gathered(weight, order):
@@ -318,38 +350,32 @@
     ups, up_layout = gathered(up_own, orders[0])
     downs, down_layout = gathered(down_own, orders[1])
 
-    def chunk_call(kernel, group, operands, outs, name, estimate):
+    def chunk_call(kernel, group, chunks, operands, outs, name, estimate):
         count = len(group)
         parts = [array(count * cap, width)] * 2
         return pl.pallas_call(
             functools.partial(kernel[0], cap, count, *kernel[1:]),
             out_shape=parts + outs,
-            in_specs=[vmem()] * (2 * count + len(operands)),
+            in_specs=[vmem()] * (len(chunks) + len(operands)),
             out_specs=[vmem()] * (2 + len(outs)),
             scratch_shapes=[pltpu.VMEM((2 * count * cap, width), BF)] * 2,
             compiler_params=params(20),
             cost_estimate=cost(estimate),
             name=name,
-        )(*[own[shift] for shift in group], *[sib[shift] for shift in group], *operands)
-
-    part_own, part_sib, near_grads, *weights = chunk_call(
-        (first_kernel, (up_layout, down_layout), n_dp),
+        )(*chunks, *operands)
+
+    total = jax.ShapeDtypeStruct((half, width), F32)
+    part_own, part_sib, *held = chunk_call(
+        (first_kernel, (up_layout, down_layout)),
         groups[0],
+        [side[shift] for side in (own, sib) for shift in groups[0]],
         [*ups, *downs],
-        [
-            array(n_dp, 2 * half, step),
-            array(width, half),
-            array(half, width),
-            array(width, half),
-        ],
+        [total, total, array(width, half), array(half, width), array(width, half)],
         "first",
-        10,
-    )
-    near_grads = lax.psum_scatter(near_grads, "dp", scatter_dimension=0, tiled=True)
+        0.1,
+    )
     halves = [(part_own, swapped(part_sib))]
-
-    own[far] = passed(own[far], 12, part_own)
-    sib[far] = swapped(own[far])
+    sums, weights = held[:2], held[2:]
 
     pairs, ready = {}, {}
 
@@ -366,19 +392,32 @@
         )(*[value for both in halves for value in both], *after)
         for shift, result in zip([shift for group in groups for shift in group], results):
             ready[shift] = result
-            pairs[shift] = passed(shifted(result, experts - shift), 20) if shift else result
-
-    paired(groups[:1], halves, own[far])
-
-    named = [ready[groups[0][-1]]]
-    part_own, part_sib, *blocks = chunk_call(
-        (late_kernel, n_dp, len(named)),
+            pairs[shift] = shifted(result, shift) if shift else result
+
+    paired(groups[:1], halves)
+
+    far_s = passed(passed(far_s, 8), 0.1, part_own)
+    last_chunk = [far_x, far_s, swapped(far_x), swapped(far_s)]
+
+    def halving(order):
+        kept = [0]
+        for bit in order[::-1]:
+            kept = [peer ^ (1 << bit) for peer in kept] + kept
+        return kept
+
+    cut = n_dp // 2
+    grads = [array(cut * half, step)] + [array(half, step)] * cut
+    part_own, part_sib, *results = chunk_call(
+        (tail_kernel, halving(orders[0]), halving(orders[1])),
         groups[1],
-        [*weights, *named],
-        [array(cap, 2 * step + 4 * half)] * n_dp,
-        "late",
-        4,
-    )
+        last_chunk,
+        [*weights, *sums, ready[groups[0][-1]]],
+        grads * 2,
+        "tail",
+        7,
+    )
+    up_grads, down_grads = results[: 1 + cut], results[1 + cut :]
+
     paired(groups[1:], [(part_own, swapped(part_sib))])
 
     grad_tokens, mark = pl.pallas_call(
@@ -391,44 +430,41 @@
         name="combine",
     )(routes_t, *[pairs[shift] for shift in range(experts)])
 
-    def to_owner(value, peer):
-        return lax.ppermute(value, "dp", [(d, d ^ peer) for d in range(n_dp)])
-
-    blocks = [
-        to_owner(passed(block, 0.1, ready[far]) if peer & (peer - 1) else block, peer)
-        if peer
-        else block
-        for peer, block in enumerate(blocks)
-    ]
-    shared = swapped(
-        pl.pallas_call(
-            share_kernel,
-            out_shape=array(n_dp * cap, 2 * step),
-            in_specs=[vmem()] * n_dp,
-            out_specs=vmem(),
-            compiler_params=params(8),
-            cost_estimate=cost(1),
-            name="share",
-        )(*blocks)
-    )
-    near_grads = near_grads[0]
-    specs = [pl.BlockSpec(near_grads.shape, lambda i: (0, 0))]
-    specs += [pl.BlockSpec(value.shape, lambda i: (0, 0)) for value in blocks + [shared]]
-    specs += [pl.BlockSpec((8, 128), lambda i: (0, 0))]
-    grad_up, grad_down = pl.pallas_call(
-        functools.partial(last_kernel, n_dp),
-        grid=(1,),
-        out_shape=[array(1, step, half)] * 2,
-        in_specs=specs,
-        out_specs=[pl.BlockSpec((1, step, half), lambda i: (0, 0, 0))] * 2,
-        scratch_shapes=[
-            pltpu.VMEM((2 * n_dp * cap, step), BF),
-            pltpu.VMEM((2 * n_dp * cap, half), BF),
-        ],
-        compiler_params=params(24),
-        cost_estimate=cost(4),
-        name="grads",
-    )(near_grads, *blocks, shared, mark)
+    def reduced(send, keeps, order, name):
+        terms = [[(keep, 0)] for keep in keeps]
+        for bit in order:
+            landed = across(send, bit)
+            for place in range(len(terms)):
+                terms[place].append((landed, place))
+            cut = len(terms) // 2
+            if cut:
+                sums = [
+                    sum(
+                        value[place * half : (place + 1) * half].astype(F32)
+                        for value, place in block
+                    ).astype(BF)
+                    for block in terms[:cut]
+                ]
+                send = jnp.concatenate(sums) if cut > 1 else sums[0]
+                terms = terms[cut:]
+        (block,) = terms
+        specs = [
+            pl.BlockSpec((half, step), functools.partial(lambda place, i: (place, 0), place))
+            for _, place in block
+        ]
+        return pl.pallas_call(
+            functools.partial(last_kernel, len(block)),
+            grid=(1,),
+            out_shape=array(1, step, half),
+            in_specs=specs + [pl.BlockSpec((8, 128), lambda i: (0, 0))],
+            out_specs=pl.BlockSpec((1, step, half), lambda i: (0, 0, 0)),
+            compiler_params=params(16),
+            cost_estimate=cost(2),
+            name=name,
+        )(*[value for value, _ in block], mark)
+
+    grad_up = reduced(up_grads[0], up_grads[1:], orders[0], "grad_up")
+    grad_down = reduced(down_grads[0], down_grads[1:], orders[1], "grad_down")
     return (grad_tokens, grad_up, grad_down)
 
 

time: 146 us -> 129 us (0.88); the launches traced: 144 us -> 129 us
  between operations: 14.1 us -> 0.79 us
  local copies, waits for them, and re-layouts: 7.38 us -> 0.03 us
  starting transfers between devices: 24.7 us -> 30.5 us
    ppermute x3 -> x0, waiting for transfers between devices: 12.8 us -> none  [to_owner(): return lax.ppermute(value, 'dp', [(d, d ^ peer) for d in range(n_dp)])]
    ppermute x4 -> x8, waiting for transfers between devices: 6.58 us -> 16.8 us  [across(): return lax.ppermute(value, 'dp', [(d, d ^ 1 << bit) for d in range(n_dp)])]
    unnamed x24 -> x12, local copies, waits for them, and re-layouts: 7.38 us -> 0.03 us
    ppermute x4 -> x8, starting transfers between devices: 5.11 us -> 10.2 us  [across(): return lax.ppermute(value, 'dp', [(d, d ^ 1 << bit) for d in range(n_dp)])]
    ppermute x6 -> x9, waiting for transfers between devices: 58.1 us -> 61.4 us  [shifted(): return lax.ppermute(value, 'expert', pairs)]
    ppermute x3 -> x0, starting transfers between devices: 1.93 us -> none  [to_owner(): return lax.ppermute(value, 'dp', [(d, d ^ peer) for d in range(n_dp)])]
    ppermute x6 -> x9, starting transfers between devices: 9.63 us -> 11.3 us  [shifted(): return lax.ppermute(value, 'expert', pairs)]
    pallas_call x2 -> x4, Pallas kernels: 2.15 us -> 3.14 us  [the longest x2 2.1 us: reduced(): pl.pallas_call(functools.partial(last_kernel, len(block)), grid=(1,), out...]
  transfers between devices with their start and end apart: 21 -> 24, of which waited for: 10 -> 6; matrix products, arithmetic and copies ran while one was open for 1% -> 0% of each run, Pallas kernels for 8% -> 11%
where the time goes in v2:
time: 129 us
  waiting for transfers between devices  79.2 us (61%)
  starting transfers between devices  30.5 us (24%)
  Pallas kernels  17.9 us (14%)
    ppermute x9, waiting for transfers between devices, shifted(): return lax.ppermute(value, 'expert', pairs)  61.4 us
    ppermute x8, waiting for transfers between devices, across(): return lax.ppermute(value, 'dp', [(d, d ^ 1 << bit) for d in range(n_dp)])  16.8 us
    ppermute x9, starting transfers between devices, shifted(): return lax.ppermute(value, 'expert', pairs)  11.3 us
    ppermute x8, starting transfers between devices, across(): return lax.ppermute(value, 'dp', [(d, d ^ 1 << bit) for d in range(n_dp)])  10.2 us
    pallas_call x2, Pallas kernels, chunk_call(): pl.pallas_call(functools.partial(kernel[0], cap, count, *kernel[1:]), out...  9.09 us
    ppermute x7, starting transfers between devices, swapped(): return lax.ppermute(value, 'expert', [(i, i ^ 1) for i in range(n_expert)])  8.93 us
    pallas_call x1, Pallas kernels, dispatch(): pl.pallas_call(functools.partial(dispatch_kernel, experts, cap, shifts, l...  3.39 us
  transfers between devices with their start and end apart: 24, of which 6 were waited for; matrix products, arithmetic and copies ran while one was open for 0% of the time, Pallas kernels for 11%

profile of v2, /device:TPU:9, one launch (start us, length us, event | category | flops | bytes accessed | tf_op | source)
XLA Modules:
  0.0 128.9 jit_solution(14490942208500773076)
XLA Ops:
  0.6 2.4 %collective-permute-start.2 = (bf16[128,2560]{1,0:T(8,128)(2,1)}, bf16[128,2560]{1,0:T(8,128)(2,1)S(1)}, u32[]{:S(2)}, u32[]{:S(2)}) collective-permute-start(bf16[128,2560]{1,0:T(8,128)(2,1)} %refs_2_.1), channel_id=1, source_target_pairs={{0,4},{1,5},{2,6},{3,7},{4,0},{5,1},{6,2},{7,3},{8,12},{9,13},{10,... | collective-permute-start | bytes 1966088 | tf_op jit(solution)/shard_map/ppermute | solution.py:260
  3.0 3.4 %dispatch.1 = (bf16[640,384]{1,0:T(8,128)(2,1)}, bf16[640,384]{1,0:T(8,128)(2,1)}, bf16[160,2560]{1,0:T(8,128)(2,1)}, bf16[160,2560]{1,0:T(8,128)(2,1)}) custom-call(s32[2,128]{1,0:T(2,128)} %bitcast.5, f32[2,128]{1,0:T(2,128)} %bitcast.7, bf16[128,2560]{1,0:T(8,128)(2,1)} %refs_2_.1, bf16[128,2560]{1,0:T(8,128)(2,1)} %cot_ref.1, bf16[640,384]{1,0:T(8,128)(2,1)} %bitcast.9, ...), custom_call_target="tpu_custom_call" | custom-call | flops 2000000000 | bytes 1048576 | tf_op jit(solution)/shard_map/dispatch/pallas_call | solution.py:271
  6.4 0.0 copy-start.1
  6.4 1.3 %collective-permute-start.10 = (bf16[640,384]{1,0:T(8,128)(2,1)}, bf16[640,384]{1,0:T(8,128)(2,1)S(1)}, u32[]{:S(2)}, u32[]{:S(2)}) collective-permute-start(bf16[640,384]{1,0:T(8,128)(2,1)} %get-tuple-element.39.refs_9_), channel_id=1, source_target_pairs={{0,16},{8,24},{16,0},{24,8},{1,17},{9,25},{17,1},{25,9},{2,18},{10... | collective-permute-start | bytes 1474568 | tf_op jit(solution)/shard_map/ppermute | solution.py:266
  7.7 1.2 collective-permute-start.8
  9.0 0.2 collective-permute-start
  9.1 0.0 copy-start
  9.2 0.1 collective-permute-start.1
  9.3 25.5 %collective-permute-done.1.plan_ref = f32[4,128]{1,0:T(4,128)S(1)} collective-permute-done((f32[4,128]{1,0:T(4,128)S(1)}, f32[4,128]{1,0:T(4,128)S(1)}, u32[]{:S(2)}, u32[]{:S(2)}) %collective-permute-start.1) | collective-permute-done | bytes 2080 | tf_op jit(solution)/shard_map/ppermute | solution.py:260
  34.8 0.0 collective-permute-done.2.tok_ref
  34.8 0.5 relay_x.1
  35.3 0.1 collective-permute-start.3
  35.4 1.9 %collective-permute-start.5 = (bf16[160,2560]{1,0:T(8,128)(2,1)S(1)}, bf16[160,2560]{1,0:T(8,128)(2,1)S(1)}, u32[]{:S(2)}, u32[]{:S(2)}) collective-permute-start(bf16[160,2560]{1,0:T(8,128)(2,1)S(1)} %copy-done.2), channel_id=1, source_target_pairs={{0,1},{1,0},{2,3},{3,2},{4,5},{5,4},{6,7},{7,6},{8,9},{9,8},{10,11... | collective-permute-start | bytes 2457608 | tf_op jit(solution)/shard_map/ppermute | solution.py:263
  37.3 0.0 collective-permute-done.10.refs_10_
  37.3 2.7 %collective-permute-start.4 = (bf16[80,2560]{1,0:T(8,128)(2,1)S(1)}, bf16[80,2560]{1,0:T(8,128)(2,1)S(1)}, u32[]{:S(2)}, u32[]{:S(2)}) collective-permute-start(bf16[80,2560]{1,0:T(8,128)(2,1)S(1)} %get-tuple-element.36), channel_id=1, source_target_pairs={{0,2},{1,3},{2,0},{3,1},{4,6},{5,7},{6,4},{7,5},{8,10},{9,11},{10,... | collective-permute-start | bytes 1228808 | tf_op jit(solution)/shard_map/ppermute | solution.py:260
  40.0 0.1 pad_maximum_fusion.1
  40.1 0.0 collective-permute-done.8.refs_7_
  40.1 1.3 collective-permute-start.11
  41.4 0.1 pad_maximum_fusion
  41.5 0.0 collective-permute-done.refs_1_
  41.5 1.3 %collective-permute-start.9 = (bf16[1280,384]{1,0:T(8,128)(2,1)S(1)}, bf16[1280,384]{1,0:T(8,128)(2,1)S(1)}, u32[]{:S(2)}, u32[]{:S(2)}) collective-permute-start(bf16[1280,384]{1,0:T(8,128)(2,1)S(1)} %pad_maximum_fusion), channel_id=1, source_target_pairs={{0,16},{8,24},{16,0},{24,8},{1,17},{9,25},{17,1},{25,9},{2,18},{10... | collective-permute-start | bytes 2949128 | tf_op jit(solution)/shard_map/ppermute | solution.py:266
  42.8 16.8 %collective-permute-done.4.named_ref.refs_0_ = bf16[80,2560]{1,0:T(8,128)(2,1)S(1)} collective-permute-done((bf16[80,2560]{1,0:T(8,128)(2,1)S(1)}, bf16[80,2560]{1,0:T(8,128)(2,1)S(1)}, u32[]{:S(2)}, u32[]{:S(2)}) %collective-permute-start.4) | collective-permute-done | bytes 409632 | tf_op jit(solution)/shard_map/ppermute | solution.py:260
  59.6 2.7 %collective-permute-start.6 = (bf16[160,2560]{1,0:T(8,128)(2,1)S(1)}, bf16[160,2560]{1,0:T(8,128)(2,1)S(1)}, u32[]{:S(2)}, u32[]{:S(2)}) collective-permute-start(bf16[160,2560]{1,0:T(8,128)(2,1)S(1)} %collective-permute-done.refs_1_), channel_id=1, source_target_pairs={{0,1},{1,0},{2,3},{3,2},{4,5},{5,4},{6,7},{7,6},{8,9},{9,8},{10,11... | collective-permute-start | bytes 2457608 | tf_op jit(solution)/shard_map/ppermute | solution.py:263
  62.3 0.0 collective-permute-done.3.cot_ref
  62.3 0.5 relay_s.1
  62.9 2.2 %collective-permute-start.7 = (bf16[160,2560]{1,0:T(8,128)(2,1)S(1)}, bf16[160,2560]{1,0:T(8,128)(2,1)S(1)}, u32[]{:S(2)}, u32[]{:S(2)}) collective-permute-start(bf16[160,2560]{1,0:T(8,128)(2,1)S(1)} %get-tuple-element.37.refs_2_), channel_id=1, source_target_pairs={{0,1},{1,0},{2,3},{3,2},{4,5},{5,4},{6,7},{7,6},{8,9},{9,8},{10,11... | collective-permute-start | bytes 2457608 | tf_op jit(solution)/shard_map/ppermute | solution.py:263
  65.0 0.0 collective-permute-done.5.refs_3_
  65.0 3.2 %collective-permute-start.15 = (bf16[80,2560]{1,0:T(8,128)(2,1)S(1)}, bf16[80,2560]{1,0:T(8,128)(2,1)S(1)}, u32[]{:S(2)}, u32[]{:S(2)}) collective-permute-start(bf16[80,2560]{1,0:T(8,128)(2,1)S(1)} %get-tuple-element.45), channel_id=1, source_target_pairs={{0,2},{1,3},{2,0},{3,1},{4,6},{5,7},{6,4},{7,5},{8,10},{9,11},{10,... | collective-permute-start | bytes 1228808 | tf_op jit(solution)/shard_map/ppermute | solution.py:260
  68.2 0.0 collective-permute-done.11.refs_11_
  68.2 0.0 collective-permute-done.9.refs_8_
  68.2 0.0 collective-permute-done.6.refs_4_
  68.2 0.0 collective-permute-done.7.refs_5_
  68.2 6.4 %first.1 = (bf16[240,2560]{1,0:T(8,128)(2,1)S(1)}, bf16[240,2560]{1,0:T(8,128)(2,1)S(1)}, f32[384,2560]{1,0:T(8,128)S(1)}, f32[384,2560]{1,0:T(8,128)S(1)}, bf16...) custom-call(bf16[160,2560]{1,0:T(8,128)(2,1)S(1)} %copy-done.2, ...), custom_call_target="tpu_custom_call" | custom-call | flops 100000000 | bytes 1048576 | tf_op jit(solution)/shard_map/first/pallas_call | solution.py:356
  74.6 0.4 collective-permute-start.12
  75.0 0.2 collective-permute-start.16
  75.2 2.8 %collective-permute-done.15.refs_0_ = bf16[80,2560]{1,0:T(8,128)(2,1)S(1)} collective-permute-done((bf16[80,2560]{1,0:T(8,128)(2,1)S(1)}, bf16[80,2560]{1,0:T(8,128)(2,1)S(1)}, u32[]{:S(2)}, u32[]{:S(2)}) %collective-permute-start.15) | collective-permute-done | bytes 409632 | tf_op jit(solution)/shard_map/ppermute | solution.py:260
  78.0 0.7 collective-permute-start.17
  78.6 0.0 collective-permute-done.12.refs_1_
  78.6 0.3 pair.2
  78.9 0.0 collective-permute-done.16.refs_2_
  78.9 1.1 collective-permute-done.17.refs_3_
  80.0 2.7 %tail.1 = (bf16[80,2560]{1,0:T(8,128)(2,1)S(1)}, bf16[80,2560]{1,0:T(8,128)(2,1)S(1)}, bf16[768,640]{1,0:T(8,128)(2,1)S(1)}, bf16[384,640]{1,0:T(8,128)(2,1)S(1)...) custom-call(bf16[80,2560]{1,0:T(8,128)(2,1)S(1)} %collective-permute, ...), custom_call_target="tpu_custom_call" | custom-call | flops 7000000000 | bytes 1048576 | tf_op jit(solution)/shard_map/tail/pallas_call | solution.py:356
  82.7 1.3 %collective-permute-start.22 = (bf16[768,640]{1,0:T(8,128)(2,1)S(1)}, bf16[768,640]{1,0:T(8,128)(2,1)S(1)}, u32[]{:S(2)}, u32[]{:S(2)}) collective-permute-start(bf16[768,640]{1,0:T(8,128)(2,1)S(1)} %get-tuple-element.59), channel_id=1, source_target_pairs={{0,16},{8,24},{16,0},{24,8},{1,17},{9,25},{17,1},{25,9},{2,18},{10... | collective-permute-start | bytes 2949128 | tf_op jit(solution)/shard_map/ppermute | solution.py:266
  84.0 1.2 collective-permute-start.20
  85.3 0.9 collective-permute-start.18
  86.2 1.4 %collective-permute-start.14 = (bf16[80,2560]{1,0:T(8,128)(2,1)S(1)}, bf16[80,2560]{1,0:T(8,128)(2,1)S(1)}, u32[]{:S(2)}, u32[]{:S(2)}) collective-permute-start(bf16[80,2560]{1,0:T(8,128)(2,1)S(1)} %get-tuple-element.44.refs_9_), channel_id=1, source_target_pairs={{0,4},{1,5},{2,6},{3,7},{4,0},{5,1},{6,2},{7,3},{8,12},{9,13},{10,... | collective-permute-start | bytes 1228808 | tf_op jit(solution)/shard_map/ppermute | solution.py:260
  87.6 0.1 collective-permute-start.13
  87.7 0.0 collective-permute-done.18.refs_1_
  87.7 0.1 pair.3
  87.8 1.2 collective-permute-start.19
  89.0 16.7 %collective-permute-done.22.refs_1_ = bf16[768,640]{1,0:T(8,128)(2,1)S(1)} collective-permute-done((bf16[768,640]{1,0:T(8,128)(2,1)S(1)}, bf16[768,640]{1,0:T(8,128)(2,1)S(1)}, u32[]{:S(2)}, u32[]{:S(2)}) %collective-permute-start.22) | collective-permute-done | bytes 983072 | tf_op jit(solution)/shard_map/ppermute | solution.py:266
  105.8 0.1 add_convert_fusion
  105.9 1.3 %collective-permute-start.23 = (bf16[384,640]{1,0:T(8,128)(2,1)S(1)}, bf16[384,640]{1,0:T(8,128)(2,1)S(1)}, u32[]{:S(2)}, u32[]{:S(2)}) collective-permute-start(bf16[384,640]{1,0:T(8,128)(2,1)S(1)} %add_convert_fusion), channel_id=1, source_target_pairs={{0,8},{8,0},{16,24},{24,16},{1,9},{9,1},{17,25},{25,17},{2,10},{10... | collective-permute-start | bytes 1474568 | tf_op jit(solution)/shard_map/ppermute | solution.py:266
  107.2 0.0 collective-permute-done.20.refs_1_
  107.2 0.1 add_convert_fusion.1
  107.3 1.3 %collective-permute-start.21 = (bf16[384,640]{1,0:T(8,128)(2,1)S(1)}, bf16[384,640]{1,0:T(8,128)(2,1)S(1)}, u32[]{:S(2)}, u32[]{:S(2)}) collective-permute-start(bf16[384,640]{1,0:T(8,128)(2,1)S(1)} %add_convert_fusion.1), channel_id=1, source_target_pairs={{0,16},{8,24},{16,0},{24,8},{1,17},{9,25},{17,1},{25,9},{2,18},{10... | collective-permute-start | bytes 1474568 | tf_op jit(solution)/shard_map/ppermute | solution.py:266
  108.6 0.0 collective-permute-done.13.rest_1_
  108.6 0.0 collective-permute-done.14.rest_2_
  108.6 16.2 %collective-permute-done.19.rest_3_ = bf16[80,2560]{1,0:T(8,128)(2,1)S(1)} collective-permute-done((bf16[80,2560]{1,0:T(8,128)(2,1)S(1)}, bf16[80,2560]{1,0:T(8,128)(2,1)S(1)}, u32[]{:S(2)}, u32[]{:S(2)}) %collective-permute-start.19) | collective-permute-done | bytes 409632 | tf_op jit(solution)/shard_map/ppermute | solution.py:260
  124.9 1.9 %combine.1 = (bf16[128,2560]{1,0:T(8,128)(2,1)}, f32[8,128]{1,0:T(8,128)S(1)}) custom-call(s32[2,128]{1,0:T(2,128)S(1)} %bitcast.6, bf16[80,2560]{1,0:T(8,128)(2,1)S(1)} %get-tuple-element.42.rest_0_, bf16[80,2560]{1,0:T(8,128)(2,1)S(1)} %collective-permute-done.13.rest_1_, bf16[80,2560]{1,0:T(8,128)(2,1)S(1)} %collective-permute-done.14.rest_2_, ...), custom_call_target="tpu_custom_call" | custom-call | flops 3000000000 | bytes 1048576 | tf_op jit(solution)/shard_map/combine/pallas_call | solution.py:423
  126.8 0.0 collective-permute-done.23.refs_2_
  126.8 1.1 grad_down.1
  127.8 0.0 collective-permute-done.21.refs_2_
  127.8 1.0 grad_up.1
  (14 shorter events, 0.0 us)
Async XLA Ops:
  0.6 34.2 %collective-permute-start.2 = (bf16[128,2560]{1,0:T(8,128)(2,1)}, bf16[128,2560]{1,0:T(8,128)(2,1)S(1)}, u32[]{:S(2)}, u32[]{:S(2)}) collective-permute-start(bf16[128,2560]{1,0:T(8,128)(2,1)} %refs_2_.1), channel_id=1, source_target_pairs={{0,4},{1,5},{2,6},{3,7},{4,0},{5,1},{6,2},{7,3},{8,12},{9,13},{10,... | collective-permute-start | bytes 1966088 | tf_op jit(solution)/shard_map/ppermute | solution.py:260
  3.0 6.1 %copy-start.3 = (s32[128,2]{0,1:T(2,128)S(1)}, s32[128,2]{0,1:T(2,128)}, u32[]{:S(2)}) copy-start(s32[128,2]{0,1:T(2,128)} %param.8) | copy-start | bytes 3076
  3.0 6.1 %copy-start.5 = (f32[128,2]{0,1:T(2,128)S(1)}, f32[128,2]{0,1:T(2,128)}, u32[]{:S(2)}) copy-start(f32[128,2]{0,1:T(2,128)} %param.9) | copy-start | bytes 3076
  3.0 31.8 %copy-start.4 = (bf16[128,2560]{1,0:T(8,128)(2,1)S(1)}, bf16[128,2560]{1,0:T(8,128)(2,1)}, u32[]{:S(2)}) copy-start(bf16[128,2560]{1,0:T(8,128)(2,1)} %cot_ref.1) | copy-start | bytes 1966084
  6.4 29.0 %copy-start.2 = (bf16[160,2560]{1,0:T(8,128)(2,1)S(1)}, bf16[160,2560]{1,0:T(8,128)(2,1)}, u32[]{:S(2)}) copy-start(bf16[160,2560]{1,0:T(8,128)(2,1)} %get-tuple-element.32.refs_0_) | copy-start | bytes 2457604
  6.4 33.5 %copy-start.1 = (bf16[640,384]{1,0:T(8,128)(2,1)S(1)}, bf16[640,384]{1,0:T(8,128)(2,1)}, u32[]{:S(2)}) copy-start(bf16[640,384]{1,0:T(8,128)(2,1)} %get-tuple-element.39.refs_9_) | copy-start | bytes 1474564
  6.4 30.9 %collective-permute-start.10 = (bf16[640,384]{1,0:T(8,128)(2,1)}, bf16[640,384]{1,0:T(8,128)(2,1)S(1)}, u32[]{:S(2)}, u32[]{:S(2)}) collective-permute-start(bf16[640,384]{1,0:T(8,128)(2,1)} %get-tuple-element.39.refs_9_), channel_id=1, source_target_pairs={{0,16},{8,24},{16,0},{24,8},{1,17},{9,25},{17,1},{25,9},{2,18},{10... | collective-permute-start | bytes 1474568 | tf_op jit(solution)/shard_map/ppermute | solution.py:266
  7.7 32.3 %collective-permute-start.8 = (bf16[640,384]{1,0:T(8,128)(2,1)}, bf16[640,384]{1,0:T(8,128)(2,1)S(1)}, u32[]{:S(2)}, u32[]{:S(2)}) collective-permute-start(bf16[640,384]{1,0:T(8,128)(2,1)} %get-tuple-element.38.refs_6_), channel_id=1, source_target_pairs={{0,8},{8,0},{16,24},{24,16},{1,9},{9,1},{17,25},{25,17},{2,10},{10... | collective-permute-start | bytes 1474568 | tf_op jit(solution)/shard_map/ppermute | solution.py:266
  9.0 32.5 %collective-permute-start = (bf16[160,2560]{1,0:T(8,128)(2,1)}, bf16[160,2560]{1,0:T(8,128)(2,1)S(1)}, u32[]{:S(2)}, u32[]{:S(2)}) collective-permute-start(bf16[160,2560]{1,0:T(8,128)(2,1)} %get-tuple-element.33), channel_id=1, source_target_pairs={{0,2},{1,3},{2,0},{3,1},{4,6},{5,7},{6,4},{7,5},{8,10},{9,11},{10,... | collective-permute-start | bytes 2457608 | tf_op jit(solution)/shard_map/ppermute | solution.py:260
  9.1 32.2 %copy-start = (bf16[640,384]{1,0:T(8,128)(2,1)S(1)}, bf16[640,384]{1,0:T(8,128)(2,1)}, u32[]{:S(2)}) copy-start(bf16[640,384]{1,0:T(8,128)(2,1)} %get-tuple-element.38.refs_6_) | copy-start | bytes 1474564
  9.2 25.6 %collective-permute-start.1 = (f32[4,128]{1,0:T(4,128)S(1)}, f32[4,128]{1,0:T(4,128)S(1)}, u32[]{:S(2)}, u32[]{:S(2)}) collective-permute-start(f32[4,128]{1,0:T(4,128)S(1)} %pad_maximum_fusion.2), channel_id=1, source_target_pairs={{0,4},{1,5},{2,6},{3,7},{4,0},{5,1},{6,2},{7,3},{8,12},{9,13},{10,... | collective-permute-start | bytes 6152 | tf_op jit(solution)/shard_map/ppermute | solution.py:260
  35.3 27.0 %collective-permute-start.3 = (bf16[128,2560]{1,0:T(8,128)(2,1)S(1)}, bf16[128,2560]{1,0:T(8,128)(2,1)S(1)}, u32[]{:S(2)}, u32[]{:S(2)}) collective-permute-start(bf16[128,2560]{1,0:T(8,128)(2,1)S(1)} %get-tuple-element.34), channel_id=1, source_target_pairs={{0,4},{1,5},{2,6},{3,7},{4,0},{5,1},{6,2},{7,3},{8,12},{9,13},{10,... | collective-permute-start | bytes 1966088 | tf_op jit(solution)/shard_map/ppermute | solution.py:260
  35.4 29.6 %collective-permute-start.5 = (bf16[160,2560]{1,0:T(8,128)(2,1)S(1)}, bf16[160,2560]{1,0:T(8,128)(2,1)S(1)}, u32[]{:S(2)}, u32[]{:S(2)}) collective-permute-start(bf16[160,2560]{1,0:T(8,128)(2,1)S(1)} %copy-done.2), channel_id=1, source_target_pairs={{0,1},{1,0},{2,3},{3,2},{4,5},{5,4},{6,7},{7,6},{8,9},{9,8},{10,11... | collective-permute-start | bytes 2457608 | tf_op jit(solution)/shard_map/ppermute | solution.py:263
  37.3 22.3 %collective-permute-start.4 = (bf16[80,2560]{1,0:T(8,128)(2,1)S(1)}, bf16[80,2560]{1,0:T(8,128)(2,1)S(1)}, u32[]{:S(2)}, u32[]{:S(2)}) collective-permute-start(bf16[80,2560]{1,0:T(8,128)(2,1)S(1)} %get-tuple-element.36), channel_id=1, source_target_pairs={{0,2},{1,3},{2,0},{3,1},{4,6},{5,7},{6,4},{7,5},{8,10},{9,11},{10,... | collective-permute-start | bytes 1228808 | tf_op jit(solution)/shard_map/ppermute | solution.py:260
  40.1 28.1 %collective-permute-start.11 = (bf16[1280,384]{1,0:T(8,128)(2,1)S(1)}, bf16[1280,384]{1,0:T(8,128)(2,1)S(1)}, u32[]{:S(2)}, u32[]{:S(2)}) collective-permute-start(bf16[1280,384]{1,0:T(8,128)(2,1)S(1)} %pad_maximum_fusion.1), channel_id=1, source_target_pairs={{0,8},{8,0},{16,24},{24,16},{1,9},{9,1},{17,25},{25,17},{2,10},{10... | collective-permute-start | bytes 2949128 | tf_op jit(solution)/shard_map/ppermute | solution.py:266
  41.5 26.8 %collective-permute-start.9 = (bf16[1280,384]{1,0:T(8,128)(2,1)S(1)}, bf16[1280,384]{1,0:T(8,128)(2,1)S(1)}, u32[]{:S(2)}, u32[]{:S(2)}) collective-permute-start(bf16[1280,384]{1,0:T(8,128)(2,1)S(1)} %pad_maximum_fusion), channel_id=1, source_target_pairs={{0,16},{8,24},{16,0},{24,8},{1,17},{9,25},{17,1},{25,9},{2,18},{10... | collective-permute-start | bytes 2949128 | tf_op jit(solution)/shard_map/ppermute | solution.py:266
  59.6 8.6 %collective-permute-start.6 = (bf16[160,2560]{1,0:T(8,128)(2,1)S(1)}, bf16[160,2560]{1,0:T(8,128)(2,1)S(1)}, u32[]{:S(2)}, u32[]{:S(2)}) collective-permute-start(bf16[160,2560]{1,0:T(8,128)(2,1)S(1)} %collective-permute-done.refs_1_), channel_id=1, source_target_pairs={{0,1},{1,0},{2,3},{3,2},{4,5},{5,4},{6,7},{7,6},{8,9},{9,8},{10,11... | collective-permute-start | bytes 2457608 | tf_op jit(solution)/shard_map/ppermute | solution.py:263
  62.9 5.4 %collective-permute-start.7 = (bf16[160,2560]{1,0:T(8,128)(2,1)S(1)}, bf16[160,2560]{1,0:T(8,128)(2,1)S(1)}, u32[]{:S(2)}, u32[]{:S(2)}) collective-permute-start(bf16[160,2560]{1,0:T(8,128)(2,1)S(1)} %get-tuple-element.37.refs_2_), channel_id=1, source_target_pairs={{0,1},{1,0},{2,3},{3,2},{4,5},{5,4},{6,7},{7,6},{8,9},{9,8},{10,11... | collective-permute-start | bytes 2457608 | tf_op jit(solution)/shard_map/ppermute | solution.py:263
  65.0 12.9 %collective-permute-start.15 = (bf16[80,2560]{1,0:T(8,128)(2,1)S(1)}, bf16[80,2560]{1,0:T(8,128)(2,1)S(1)}, u32[]{:S(2)}, u32[]{:S(2)}) collective-permute-start(bf16[80,2560]{1,0:T(8,128)(2,1)S(1)} %get-tuple-element.45), channel_id=1, source_target_pairs={{0,2},{1,3},{2,0},{3,1},{4,6},{5,7},{6,4},{7,5},{8,10},{9,11},{10,... | collective-permute-start | bytes 1228808 | tf_op jit(solution)/shard_map/ppermute | solution.py:260
  74.6 4.0 %collective-permute-start.12 = (bf16[240,2560]{1,0:T(8,128)(2,1)S(1)}, bf16[240,2560]{1,0:T(8,128)(2,1)S(1)}, u32[]{:S(2)}, u32[]{:S(2)}) collective-permute-start(bf16[240,2560]{1,0:T(8,128)(2,1)S(1)} %get-tuple-element.41), channel_id=1, source_target_pairs={{0,1},{1,0},{2,3},{3,2},{4,5},{5,4},{6,7},{7,6},{8,9},{9,8},{10,11... | collective-permute-start | bytes 3686408 | tf_op jit(solution)/shard_map/ppermute | solution.py:263
  75.0 3.9 %collective-permute-start.16 = (bf16[80,2560]{1,0:T(8,128)(2,1)S(1)}, bf16[80,2560]{1,0:T(8,128)(2,1)S(1)}, u32[]{:S(2)}, u32[]{:S(2)}) collective-permute-start(bf16[80,2560]{1,0:T(8,128)(2,1)S(1)} %collective-permute-done.4.named_ref.refs_0_), channel_id=1, source_target_pairs={{0,1},{1,0},{2,3},{3,2},{4,5},{5,4},{6,7},{7,6},{8,9},{9,8},{10,11... | collective-permute-start | bytes 1228808 | tf_op jit(solution)/shard_map/ppermute | solution.py:263
  78.0 2.0 %collective-permute-start.17 = (bf16[80,2560]{1,0:T(8,128)(2,1)S(1)}, bf16[80,2560]{1,0:T(8,128)(2,1)S(1)}, u32[]{:S(2)}, u32[]{:S(2)}) collective-permute-start(bf16[80,2560]{1,0:T(8,128)(2,1)S(1)} %after.3.refs_1_), channel_id=1, source_target_pairs={{0,1},{1,0},{2,3},{3,2},{4,5},{5,4},{6,7},{7,6},{8,9},{9,8},{10,11... | collective-permute-start | bytes 1228808 | tf_op jit(solution)/shard_map/ppermute | solution.py:263
  82.7 23.0 %collective-permute-start.22 = (bf16[768,640]{1,0:T(8,128)(2,1)S(1)}, bf16[768,640]{1,0:T(8,128)(2,1)S(1)}, u32[]{:S(2)}, u32[]{:S(2)}) collective-permute-start(bf16[768,640]{1,0:T(8,128)(2,1)S(1)} %get-tuple-element.59), channel_id=1, source_target_pairs={{0,16},{8,24},{16,0},{24,8},{1,17},{9,25},{17,1},{25,9},{2,18},{10... | collective-permute-start | bytes 2949128 | tf_op jit(solution)/shard_map/ppermute | solution.py:266
  84.0 23.1 %collective-permute-start.20 = (bf16[768,640]{1,0:T(8,128)(2,1)S(1)}, bf16[768,640]{1,0:T(8,128)(2,1)S(1)}, u32[]{:S(2)}, u32[]{:S(2)}) collective-permute-start(bf16[768,640]{1,0:T(8,128)(2,1)S(1)} %get-tuple-element.55), channel_id=1, source_target_pairs={{0,8},{8,0},{16,24},{24,16},{1,9},{9,1},{17,25},{25,17},{2,10},{10... | collective-permute-start | bytes 2949128 | tf_op jit(solution)/shard_map/ppermute | solution.py:266
  85.3 2.4 %collective-permute-start.18 = (bf16[80,2560]{1,0:T(8,128)(2,1)S(1)}, bf16[80,2560]{1,0:T(8,128)(2,1)S(1)}, u32[]{:S(2)}, u32[]{:S(2)}) collective-permute-start(bf16[80,2560]{1,0:T(8,128)(2,1)S(1)} %get-tuple-element.52), channel_id=1, source_target_pairs={{0,1},{1,0},{2,3},{3,2},{4,5},{5,4},{6,7},{7,6},{8,9},{9,8},{10,11... | collective-permute-start | bytes 1228808 | tf_op jit(solution)/shard_map/ppermute | solution.py:263
  86.2 22.4 %collective-permute-start.14 = (bf16[80,2560]{1,0:T(8,128)(2,1)S(1)}, bf16[80,2560]{1,0:T(8,128)(2,1)S(1)}, u32[]{:S(2)}, u32[]{:S(2)}) collective-permute-start(bf16[80,2560]{1,0:T(8,128)(2,1)S(1)} %get-tuple-element.44.refs_9_), channel_id=1, source_target_pairs={{0,4},{1,5},{2,6},{3,7},{4,0},{5,1},{6,2},{7,3},{8,12},{9,13},{10,... | collective-permute-start | bytes 1228808 | tf_op jit(solution)/shard_map/ppermute | solution.py:260
  87.6 21.0 %collective-permute-start.13 = (bf16[80,2560]{1,0:T(8,128)(2,1)S(1)}, bf16[80,2560]{1,0:T(8,128)(2,1)S(1)}, u32[]{:S(2)}, u32[]{:S(2)}) collective-permute-start(bf16[80,2560]{1,0:T(8,128)(2,1)S(1)} %get-tuple-element.43), channel_id=1, source_target_pairs={{0,2},{1,3},{2,0},{3,1},{4,6},{5,7},{6,4},{7,5},{8,10},{9,11},{10,... | collective-permute-start | bytes 1228808 | tf_op jit(solution)/shard_map/ppermute | solution.py:260
  87.8 37.1 %collective-permute-start.19 = (bf16[80,2560]{1,0:T(8,128)(2,1)S(1)}, bf16[80,2560]{1,0:T(8,128)(2,1)S(1)}, u32[]{:S(2)}, u32[]{:S(2)}) collective-permute-start(bf16[80,2560]{1,0:T(8,128)(2,1)S(1)} %pair.3), channel_id=1, source_target_pairs={{0,6},{1,7},{2,4},{3,5},{4,2},{5,3},{6,0},{7,1},{8,14},{9,15},{10,... | collective-permute-start | bytes 1228808 | tf_op jit(solution)/shard_map/ppermute | solution.py:260
  105.9 20.9 %collective-permute-start.23 = (bf16[384,640]{1,0:T(8,128)(2,1)S(1)}, bf16[384,640]{1,0:T(8,128)(2,1)S(1)}, u32[]{:S(2)}, u32[]{:S(2)}) collective-permute-start(bf16[384,640]{1,0:T(8,128)(2,1)S(1)} %add_convert_fusion), channel_id=1, source_target_pairs={{0,8},{8,0},{16,24},{24,16},{1,9},{9,1},{17,25},{25,17},{2,10},{10... | collective-permute-start | bytes 1474568 | tf_op jit(solution)/shard_map/ppermute | solution.py:266
  107.3 20.5 %collective-permute-start.21 = (bf16[384,640]{1,0:T(8,128)(2,1)S(1)}, bf16[384,640]{1,0:T(8,128)(2,1)S(1)}, u32[]{:S(2)}, u32[]{:S(2)}) collective-permute-start(bf16[384,640]{1,0:T(8,128)(2,1)S(1)} %add_convert_fusion.1), channel_id=1, source_target_pairs={{0,16},{8,24},{16,0},{24,8},{1,17},{9,25},{17,1},{25,9},{2,18},{10... | collective-permute-start | bytes 1474568 | tf_op jit(solution)/shard_map/ppermute | solution.py:266

commit v3 on v2

--- a/solution.py
+++ b/solution.py
@@ -306,8 +306,10 @@
     relayed = experts == 4
     order = [1, 0] if relayed else shifts[1:] + [0]
     up_own, down_own, *sends = dispatch(order, up_weight[0], down_weight[0])
-    for shift, send in zip(order, sends):
-        own[shift] = shifted(send, shift) if shift else send
+    sends = dict(zip(order, sends))
+    for shift in order:
+        if shift != 1:
+            own[shift] = shifted(sends[shift], shift) if shift else sends[shift]
     if relayed:
         plan = shifted(jnp.concatenate([routes_t.astype(F32), gates_t]), 2)
         landed = shifted(tokens, 2)
@@ -334,9 +336,6 @@
         far_s = shifted(on_s, 1)
     else:
         far_x, far_s = own[experts - 1][:cap], own[experts - 1][cap:]
-    for shift in groups[0]:
-        sib[shift] = swapped(own[shift])
-
     def gathered(weight, order):
         blocks, layout, held = [weight], [[0]], [0]
         for bit in order:
@@ -349,6 +348,10 @@
 
     ups, up_layout = gathered(up_own, orders[0])
     downs, down_layout = gathered(down_own, orders[1])
+    own[1] = shifted(passed(sends[1], 0.1, ups[1]), 1)
+    for shift in groups[0]:
+        sib[shift] = swapped(own[shift])
+    ups[-1], downs[-1] = passed(ups[-1], 3), passed(downs[-1], 3)
 
     def chunk_call(kernel, group, chunks, operands, outs, name, estimate):
         count = len(group)

time: 129 us -> 137 us (1.062)
  waiting for transfers between devices: 79.2 us -> 88.8 us
  starting transfers between devices: 30.5 us -> 25.8 us
  local copies, waits for them, and re-layouts: 0.03 us -> 2.07 us
    ppermute x8, waiting for transfers between devices: 16.8 us -> 24.5 us  [across(): return lax.ppermute(value, 'dp', [(d, d ^ 1 << bit) for d in range(n_dp)])]
    ppermute x7, starting transfers between devices: 8.93 us -> 3.24 us  [swapped(): return lax.ppermute(value, 'expert', [(i, i ^ 1) for i in range(n_expert)])]
    unnamed x12 -> x16, local copies, waits for them, and re-layouts: 0.03 us -> 2.07 us
  transfers between devices with their start and end apart: 24 -> 24, of which waited for: 6 -> 9; matrix products, arithmetic and copies ran while one was open for 0% -> 0% of each run, Pallas kernels for 11% -> 10%
where the time goes in v3:
time: 137 us; the launch traced here: 136 us
  waiting for transfers between devices  88.8 us (65%)
  starting transfers between devices  25.8 us (19%)
  Pallas kernels  17.9 us (13%)
  local copies, waits for them, and re-layouts  2.07 us (2%)
    ppermute x9, waiting for transfers between devices, shifted(): return lax.ppermute(value, 'expert', pairs)  62.3 us
    ppermute x8, waiting for transfers between devices, across(): return lax.ppermute(value, 'dp', [(d, d ^ 1 << bit) for d in range(n_dp)])  24.5 us
    ppermute x9, starting transfers between devices, shifted(): return lax.ppermute(value, 'expert', pairs)  12.3 us
    ppermute x8, starting transfers between devices, across(): return lax.ppermute(value, 'dp', [(d, d ^ 1 << bit) for d in range(n_dp)])  10.3 us
    pallas_call x2, Pallas kernels, chunk_call(): pl.pallas_call(functools.partial(kernel[0], cap, count, *kernel[1:]), out...  9.08 us
    pallas_call x1, Pallas kernels, dispatch(): pl.pallas_call(functools.partial(dispatch_kernel, experts, cap, shifts, l...  3.39 us
    ppermute x7, starting transfers between devices, swapped(): return lax.ppermute(value, 'expert', [(i, i ^ 1) for i in range(n_expert)])  3.24 us
  transfers between devices with their start and end apart: 24, of which 9 were waited for; matrix products, arithmetic and copies ran while one was open for 0% of the time, Pallas kernels for 10%

profile of v3, /device:TPU:9, one launch (start us, length us, event | category | flops | bytes accessed | tf_op | source)
XLA Modules:
  0.0 135.9 jit_solution(17442736428319798462)
XLA Ops:
  0.6 2.4 %collective-permute-start.3 = (bf16[128,2560]{1,0:T(8,128)(2,1)}, bf16[128,2560]{1,0:T(8,128)(2,1)S(1)}, u32[]{:S(2)}, u32[]{:S(2)}) collective-permute-start(bf16[128,2560]{1,0:T(8,128)(2,1)} %refs_2_.1), channel_id=1, source_target_pairs={{0,4},{1,5},{2,6},{3,7},{4,0},{5,1},{6,2},{7,3},{8,12},{9,13},{10,... | collective-permute-start | bytes 1966088 | tf_op jit(solution)/shard_map/ppermute | solution.py:260
  3.0 3.4 %dispatch.1 = (bf16[640,384]{1,0:T(8,128)(2,1)}, bf16[640,384]{1,0:T(8,128)(2,1)}, bf16[160,2560]{1,0:T(8,128)(2,1)}, bf16[160,2560]{1,0:T(8,128)(2,1)}) custom-call(s32[2,128]{1,0:T(2,128)} %bitcast.5, f32[2,128]{1,0:T(2,128)} %bitcast.7, bf16[128,2560]{1,0:T(8,128)(2,1)} %refs_2_.1, bf16[128,2560]{1,0:T(8,128)(2,1)} %cot_ref.1, bf16[640,384]{1,0:T(8,128)(2,1)} %bitcast.9, ...), custom_call_target="tpu_custom_call" | custom-call | flops 2000000000 | bytes 1048576 | tf_op jit(solution)/shard_map/dispatch/pallas_call | solution.py:271
  6.4 1.3 collective-permute-start
  7.7 1.2 collective-permute-start.10
  8.9 0.1 collective-permute-start.2
  9.1 9.4 %collective-permute-done.refs_1_.refs_7_ = bf16[640,384]{1,0:T(8,128)(2,1)S(1)} collective-permute-done((bf16[640,384]{1,0:T(8,128)(2,1)}, bf16[640,384]{1,0:T(8,128)(2,1)S(1)}, u32[]{:S(2)}, u32[]{:S(2)}) %collective-permute-start) | collective-permute-done | bytes 491552 | tf_op jit(solution)/shard_map/ppermute | solution.py:266
  18.5 1.1 copy-done.3
  19.6 0.9 copy-done.4
  20.5 0.2 collective-permute-start.1
  20.7 11.1 %collective-permute-done.2.plan_ref = f32[4,128]{1,0:T(4,128)S(1)} collective-permute-done((f32[4,128]{1,0:T(4,128)S(1)}, f32[4,128]{1,0:T(4,128)S(1)}, u32[]{:S(2)}, u32[]{:S(2)}) %collective-permute-start.2) | collective-permute-done | bytes 2080 | tf_op jit(solution)/shard_map/ppermute | solution.py:260
  31.8 0.0 collective-permute-done.3.tok_ref
  31.8 0.5 relay_x.1
  32.3 3.1 %collective-permute-start.4 = (bf16[128,2560]{1,0:T(8,128)(2,1)S(1)}, bf16[128,2560]{1,0:T(8,128)(2,1)S(1)}, u32[]{:S(2)}, u32[]{:S(2)}) collective-permute-start(bf16[128,2560]{1,0:T(8,128)(2,1)S(1)} %get-tuple-element.35), channel_id=1, source_target_pairs={{0,4},{1,5},{2,6},{3,7},{4,0},{5,1},{6,2},{7,3},{8,12},{9,13},{10,... | collective-permute-start | bytes 1966088 | tf_op jit(solution)/shard_map/ppermute | solution.py:260
  35.4 0.1 pad_maximum_fusion
  35.5 1.3 collective-permute-start.9
  36.8 0.0 collective-permute-start.5
  36.9 0.0 collective-permute-done.10.refs_10_
  36.9 0.1 pad_maximum_fusion.1
  37.0 1.3 collective-permute-start.11
  38.3 32.6 %collective-permute-done.5.named_ref.refs_0_ = bf16[80,2560]{1,0:T(8,128)(2,1)S(1)} collective-permute-done((bf16[80,2560]{1,0:T(8,128)(2,1)S(1)}, bf16[80,2560]{1,0:T(8,128)(2,1)S(1)}, u32[]{:S(2)}, u32[]{:S(2)}) %collective-permute-start.5) | collective-permute-done | bytes 409632 | tf_op jit(solution)/shard_map/ppermute | solution.py:260
  70.9 0.5 collective-permute-start.6
  71.4 0.0 collective-permute-done.4.cot_ref
  71.4 0.5 relay_s.1
  71.9 0.1 collective-permute-start.8
  72.0 0.0 collective-permute-done.1.refs_1_
  72.0 0.5 collective-permute-start.7
  72.5 0.0 collective-permute-done.9.refs_0_
  72.5 2.2 %collective-permute-start.15 = (bf16[80,2560]{1,0:T(8,128)(2,1)S(1)}, bf16[80,2560]{1,0:T(8,128)(2,1)S(1)}, u32[]{:S(2)}, u32[]{:S(2)}) collective-permute-start(bf16[80,2560]{1,0:T(8,128)(2,1)S(1)} %get-tuple-element.45), channel_id=1, source_target_pairs={{0,2},{1,3},{2,0},{3,1},{4,6},{5,7},{6,4},{7,5},{8,10},{9,11},{10,... | collective-permute-start | bytes 1228808 | tf_op jit(solution)/shard_map/ppermute | solution.py:260
  74.7 0.0 collective-permute-done.11.refs_0_
  74.7 0.0 collective-permute-done.6.refs_3_
  74.7 0.0 collective-permute-done.8.refs_5_
  74.7 1.0 collective-permute-done.7.refs_4_
  75.7 6.4 %first.1 = (bf16[240,2560]{1,0:T(8,128)(2,1)S(1)}, bf16[240,2560]{1,0:T(8,128)(2,1)S(1)}, f32[384,2560]{1,0:T(8,128)S(1)}, f32[384,2560]{1,0:T(8,128)S(1)}, bf16...) custom-call(bf16[160,2560]{1,0:T(8,128)(2,1)S(1)} %copy-done.2, ...), custom_call_target="tpu_custom_call" | custom-call | flops 100000000 | bytes 1048576 | tf_op jit(solution)/shard_map/first/pallas_call | solution.py:359
  82.0 0.4 collective-permute-start.12
  82.5 0.1 collective-permute-start.16
  82.6 1.8 %collective-permute-done.15.refs_0_ = bf16[80,2560]{1,0:T(8,128)(2,1)S(1)} collective-permute-done((bf16[80,2560]{1,0:T(8,128)(2,1)S(1)}, bf16[80,2560]{1,0:T(8,128)(2,1)S(1)}, u32[]{:S(2)}, u32[]{:S(2)}) %collective-permute-start.15) | collective-permute-done | bytes 409632 | tf_op jit(solution)/shard_map/ppermute | solution.py:260
  84.5 0.7 collective-permute-start.17
  85.1 0.0 collective-permute-done.12.refs_1_
  85.1 0.3 pair.2
  85.4 0.2 collective-permute-done.16.refs_2_
  85.6 0.9 collective-permute-done.17.refs_3_
  86.5 2.7 %tail.1 = (bf16[80,2560]{1,0:T(8,128)(2,1)S(1)}, bf16[80,2560]{1,0:T(8,128)(2,1)S(1)}, bf16[768,640]{1,0:T(8,128)(2,1)S(1)}, bf16[384,640]{1,0:T(8,128)(2,1)S(1)...) custom-call(bf16[80,2560]{1,0:T(8,128)(2,1)S(1)} %collective-permute, ...), custom_call_target="tpu_custom_call" | custom-call | flops 7000000000 | bytes 1048576 | tf_op jit(solution)/shard_map/tail/pallas_call | solution.py:359
  89.2 1.4 %collective-permute-start.22 = (bf16[768,640]{1,0:T(8,128)(2,1)S(1)}, bf16[768,640]{1,0:T(8,128)(2,1)S(1)}, u32[]{:S(2)}, u32[]{:S(2)}) collective-permute-start(bf16[768,640]{1,0:T(8,128)(2,1)S(1)} %get-tuple-element.59), channel_id=1, source_target_pairs={{0,16},{8,24},{16,0},{24,8},{1,17},{9,25},{17,1},{25,9},{2,18},{10... | collective-permute-start | bytes 2949128 | tf_op jit(solution)/shard_map/ppermute | solution.py:266
  90.6 1.2 collective-permute-start.20
  91.8 0.9 collective-permute-start.18
  92.7 3.9 %collective-permute-start.14 = (bf16[80,2560]{1,0:T(8,128)(2,1)S(1)}, bf16[80,2560]{1,0:T(8,128)(2,1)S(1)}, u32[]{:S(2)}, u32[]{:S(2)}) collective-permute-start(bf16[80,2560]{1,0:T(8,128)(2,1)S(1)} %get-tuple-element.44.refs_9_), channel_id=1, source_target_pairs={{0,4},{1,5},{2,6},{3,7},{4,0},{5,1},{6,2},{7,3},{8,12},{9,13},{10,... | collective-permute-start | bytes 1228808 | tf_op jit(solution)/shard_map/ppermute | solution.py:260
  96.7 0.0 collective-permute-start.13
  96.7 0.0 collective-permute-done.18.refs_1_
  96.7 0.1 pair.3
  96.8 0.3 collective-permute-start.19
  97.1 15.1 %collective-permute-done.22.refs_1_ = bf16[768,640]{1,0:T(8,128)(2,1)S(1)} collective-permute-done((bf16[768,640]{1,0:T(8,128)(2,1)S(1)}, bf16[768,640]{1,0:T(8,128)(2,1)S(1)}, u32[]{:S(2)}, u32[]{:S(2)}) %collective-permute-start.22) | collective-permute-done | bytes 983072 | tf_op jit(solution)/shard_map/ppermute | solution.py:266
  112.3 0.1 add_convert_fusion
  112.4 1.3 collective-permute-start.23
  113.7 0.0 collective-permute-done.20.refs_1_
  113.7 0.1 add_convert_fusion.1
  113.9 1.3 collective-permute-start.21
  115.2 0.0 collective-permute-done.13.rest_1_
  115.2 0.0 collective-permute-done.14.rest_2_
  115.2 16.7 %collective-permute-done.19.rest_3_ = bf16[80,2560]{1,0:T(8,128)(2,1)S(1)} collective-permute-done((bf16[80,2560]{1,0:T(8,128)(2,1)S(1)}, bf16[80,2560]{1,0:T(8,128)(2,1)S(1)}, u32[]{:S(2)}, u32[]{:S(2)}) %collective-permute-start.19) | collective-permute-done | bytes 409632 | tf_op jit(solution)/shard_map/ppermute | solution.py:260
  131.8 1.9 %combine.1 = (bf16[128,2560]{1,0:T(8,128)(2,1)}, f32[8,128]{1,0:T(8,128)S(1)}) custom-call(s32[2,128]{1,0:T(2,128)S(1)} %bitcast.6, bf16[80,2560]{1,0:T(8,128)(2,1)S(1)} %get-tuple-element.42.rest_0_, bf16[80,2560]{1,0:T(8,128)(2,1)S(1)} %collective-permute-done.13.rest_1_, bf16[80,2560]{1,0:T(8,128)(2,1)S(1)} %collective-permute-done.14.rest_2_, ...), custom_call_target="tpu_custom_call" | custom-call | flops 3000000000 | bytes 1048576 | tf_op jit(solution)/shard_map/combine/pallas_call | solution.py:426
  133.8 0.0 collective-permute-done.23.refs_2_
  133.8 1.1 grad_down.1
  134.8 0.0 collective-permute-done.21.refs_2_
  134.8 1.1 grad_up.1
  (21 shorter events, 0.0 us)
Async XLA Ops:
  0.6 31.2 %collective-permute-start.3 = (bf16[128,2560]{1,0:T(8,128)(2,1)}, bf16[128,2560]{1,0:T(8,128)(2,1)S(1)}, u32[]{:S(2)}, u32[]{:S(2)}) collective-permute-start(bf16[128,2560]{1,0:T(8,128)(2,1)} %refs_2_.1), channel_id=1, source_target_pairs={{0,4},{1,5},{2,6},{3,7},{4,0},{5,1},{6,2},{7,3},{8,12},{9,13},{10,... | collective-permute-start | bytes 1966088 | tf_op jit(solution)/shard_map/ppermute | solution.py:260
  3.0 5.9 %copy-start.5 = (s32[128,2]{0,1:T(2,128)S(1)}, s32[128,2]{0,1:T(2,128)}, u32[]{:S(2)}) copy-start(s32[128,2]{0,1:T(2,128)} %param.8) | copy-start | bytes 3076
  3.0 5.9 %copy-start.7 = (f32[128,2]{0,1:T(2,128)S(1)}, f32[128,2]{0,1:T(2,128)}, u32[]{:S(2)}) copy-start(f32[128,2]{0,1:T(2,128)} %param.9) | copy-start | bytes 3076
  3.0 28.8 %copy-start.6 = (bf16[128,2560]{1,0:T(8,128)(2,1)S(1)}, bf16[128,2560]{1,0:T(8,128)(2,1)}, u32[]{:S(2)}) copy-start(bf16[128,2560]{1,0:T(8,128)(2,1)} %cot_ref.1) | copy-start | bytes 1966084
  6.4 12.0 %collective-permute-start = (bf16[640,384]{1,0:T(8,128)(2,1)}, bf16[640,384]{1,0:T(8,128)(2,1)S(1)}, u32[]{:S(2)}, u32[]{:S(2)}) collective-permute-start(bf16[640,384]{1,0:T(8,128)(2,1)} %get-tuple-element.34.refs_6_), channel_id=1, source_target_pairs={{0,8},{8,0},{16,24},{24,16},{1,9},{9,1},{17,25},{25,17},{2,10},{10... | collective-permute-start | bytes 1474568 | tf_op jit(solution)/shard_map/ppermute | solution.py:266
  7.7 29.2 %collective-permute-start.10 = (bf16[640,384]{1,0:T(8,128)(2,1)}, bf16[640,384]{1,0:T(8,128)(2,1)S(1)}, u32[]{:S(2)}, u32[]{:S(2)}) collective-permute-start(bf16[640,384]{1,0:T(8,128)(2,1)} %get-tuple-element.39.refs_9_), channel_id=1, source_target_pairs={{0,16},{8,24},{16,0},{24,8},{1,17},{9,25},{17,1},{25,9},{2,18},{10... | collective-permute-start | bytes 1474568 | tf_op jit(solution)/shard_map/ppermute | solution.py:266
  8.9 22.8 %collective-permute-start.2 = (f32[4,128]{1,0:T(4,128)S(1)}, f32[4,128]{1,0:T(4,128)S(1)}, u32[]{:S(2)}, u32[]{:S(2)}) collective-permute-start(f32[4,128]{1,0:T(4,128)S(1)} %pad_maximum_fusion.2), channel_id=1, source_target_pairs={{0,4},{1,5},{2,6},{3,7},{4,0},{5,1},{6,2},{7,3},{8,12},{9,13},{10,... | collective-permute-start | bytes 6152 | tf_op jit(solution)/shard_map/ppermute | solution.py:260
  18.5 1.1 copy-start.3
  19.6 0.9 copy-start.4
  20.5 14.9 %copy-start = (bf16[640,384]{1,0:T(8,128)(2,1)S(1)}, bf16[640,384]{1,0:T(8,128)(2,1)}, u32[]{:S(2)}) copy-start(bf16[640,384]{1,0:T(8,128)(2,1)} %get-tuple-element.34.refs_6_) | copy-start | bytes 1474564
  20.5 16.4 %copy-start.1 = (bf16[640,384]{1,0:T(8,128)(2,1)S(1)}, bf16[640,384]{1,0:T(8,128)(2,1)}, u32[]{:S(2)}) copy-start(bf16[640,384]{1,0:T(8,128)(2,1)} %get-tuple-element.39.refs_9_) | copy-start | bytes 1474564
  20.5 51.5 %collective-permute-start.1 = (bf16[160,2560]{1,0:T(8,128)(2,1)}, bf16[160,2560]{1,0:T(8,128)(2,1)S(1)}, u32[]{:S(2)}, u32[]{:S(2)}) collective-permute-start(bf16[160,2560]{1,0:T(8,128)(2,1)} %copy-done.4), channel_id=1, source_target_pairs={{0,2},{1,3},{2,0},{3,1},{4,6},{5,7},{6,4},{7,5},{8,10},{9,11},{10,... | collective-permute-start | bytes 2457608 | tf_op jit(solution)/shard_map/ppermute | solution.py:260
  32.3 38.6 %copy-start.2 = (bf16[160,2560]{1,0:T(8,128)(2,1)S(1)}, bf16[160,2560]{1,0:T(8,128)(2,1)}, u32[]{:S(2)}) copy-start(bf16[160,2560]{1,0:T(8,128)(2,1)} %get-tuple-element.32.refs_0_) | copy-start | bytes 2457604
  32.3 39.1 %collective-permute-start.4 = (bf16[128,2560]{1,0:T(8,128)(2,1)S(1)}, bf16[128,2560]{1,0:T(8,128)(2,1)S(1)}, u32[]{:S(2)}, u32[]{:S(2)}) collective-permute-start(bf16[128,2560]{1,0:T(8,128)(2,1)S(1)} %get-tuple-element.35), channel_id=1, source_target_pairs={{0,4},{1,5},{2,6},{3,7},{4,0},{5,1},{6,2},{7,3},{8,12},{9,13},{10,... | collective-permute-start | bytes 1966088 | tf_op jit(solution)/shard_map/ppermute | solution.py:260
  35.5 37.0 %collective-permute-start.9 = (bf16[1280,384]{1,0:T(8,128)(2,1)S(1)}, bf16[1280,384]{1,0:T(8,128)(2,1)S(1)}, u32[]{:S(2)}, u32[]{:S(2)}) collective-permute-start(bf16[1280,384]{1,0:T(8,128)(2,1)S(1)} %pad_maximum_fusion), channel_id=1, source_target_pairs={{0,16},{8,24},{16,0},{24,8},{1,17},{9,25},{17,1},{25,9},{2,18},{10... | collective-permute-start | bytes 2949128 | tf_op jit(solution)/shard_map/ppermute | solution.py:266
  36.8 34.0 %collective-permute-start.5 = (bf16[80,2560]{1,0:T(8,128)(2,1)S(1)}, bf16[80,2560]{1,0:T(8,128)(2,1)S(1)}, u32[]{:S(2)}, u32[]{:S(2)}) collective-permute-start(bf16[80,2560]{1,0:T(8,128)(2,1)S(1)} %get-tuple-element.37), channel_id=1, source_target_pairs={{0,2},{1,3},{2,0},{3,1},{4,6},{5,7},{6,4},{7,5},{8,10},{9,11},{10,... | collective-permute-start | bytes 1228808 | tf_op jit(solution)/shard_map/ppermute | solution.py:260
  37.0 37.7 %collective-permute-start.11 = (bf16[1280,384]{1,0:T(8,128)(2,1)S(1)}, bf16[1280,384]{1,0:T(8,128)(2,1)S(1)}, u32[]{:S(2)}, u32[]{:S(2)}) collective-permute-start(bf16[1280,384]{1,0:T(8,128)(2,1)S(1)} %pad_maximum_fusion.1), channel_id=1, source_target_pairs={{0,8},{8,0},{16,24},{24,16},{1,9},{9,1},{17,25},{25,17},{2,10},{10... | collective-permute-start | bytes 2949128 | tf_op jit(solution)/shard_map/ppermute | solution.py:266
  70.9 3.8 %collective-permute-start.6 = (bf16[160,2560]{1,0:T(8,128)(2,1)S(1)}, bf16[160,2560]{1,0:T(8,128)(2,1)S(1)}, u32[]{:S(2)}, u32[]{:S(2)}) collective-permute-start(bf16[160,2560]{1,0:T(8,128)(2,1)S(1)} %copy-done.2), channel_id=1, source_target_pairs={{0,1},{1,0},{2,3},{3,2},{4,5},{5,4},{6,7},{7,6},{8,9},{9,8},{10,11... | collective-permute-start | bytes 2457608 | tf_op jit(solution)/shard_map/ppermute | solution.py:263
  71.9 2.8 %collective-permute-start.8 = (bf16[160,2560]{1,0:T(8,128)(2,1)S(1)}, bf16[160,2560]{1,0:T(8,128)(2,1)S(1)}, u32[]{:S(2)}, u32[]{:S(2)}) collective-permute-start(bf16[160,2560]{1,0:T(8,128)(2,1)S(1)} %get-tuple-element.38.refs_2_), channel_id=1, source_target_pairs={{0,1},{1,0},{2,3},{3,2},{4,5},{5,4},{6,7},{7,6},{8,9},{9,8},{10,11... | collective-permute-start | bytes 2457608 | tf_op jit(solution)/shard_map/ppermute | solution.py:263
  72.0 3.7 %collective-permute-start.7 = (bf16[160,2560]{1,0:T(8,128)(2,1)S(1)}, bf16[160,2560]{1,0:T(8,128)(2,1)S(1)}, u32[]{:S(2)}, u32[]{:S(2)}) collective-permute-start(bf16[160,2560]{1,0:T(8,128)(2,1)S(1)} %collective-permute-done.1.refs_1_), channel_id=1, source_target_pairs={{0,1},{1,0},{2,3},{3,2},{4,5},{5,4},{6,7},{7,6},{8,9},{9,8},{10,11... | collective-permute-start | bytes 2457608 | tf_op jit(solution)/shard_map/ppermute | solution.py:263
  72.5 12.0 %collective-permute-start.15 = (bf16[80,2560]{1,0:T(8,128)(2,1)S(1)}, bf16[80,2560]{1,0:T(8,128)(2,1)S(1)}, u32[]{:S(2)}, u32[]{:S(2)}) collective-permute-start(bf16[80,2560]{1,0:T(8,128)(2,1)S(1)} %get-tuple-element.45), channel_id=1, source_target_pairs={{0,2},{1,3},{2,0},{3,1},{4,6},{5,7},{6,4},{7,5},{8,10},{9,11},{10,... | collective-permute-start | bytes 1228808 | tf_op jit(solution)/shard_map/ppermute | solution.py:260
  82.0 3.1 %collective-permute-start.12 = (bf16[240,2560]{1,0:T(8,128)(2,1)S(1)}, bf16[240,2560]{1,0:T(8,128)(2,1)S(1)}, u32[]{:S(2)}, u32[]{:S(2)}) collective-permute-start(bf16[240,2560]{1,0:T(8,128)(2,1)S(1)} %get-tuple-element.41), channel_id=1, source_target_pairs={{0,1},{1,0},{2,3},{3,2},{4,5},{5,4},{6,7},{7,6},{8,9},{9,8},{10,11... | collective-permute-start | bytes 3686408 | tf_op jit(solution)/shard_map/ppermute | solution.py:263
  82.5 3.1 %collective-permute-start.16 = (bf16[80,2560]{1,0:T(8,128)(2,1)S(1)}, bf16[80,2560]{1,0:T(8,128)(2,1)S(1)}, u32[]{:S(2)}, u32[]{:S(2)}) collective-permute-start(bf16[80,2560]{1,0:T(8,128)(2,1)S(1)} %collective-permute-done.5.named_ref.refs_0_), channel_id=1, source_target_pairs={{0,1},{1,0},{2,3},{3,2},{4,5},{5,4},{6,7},{7,6},{8,9},{9,8},{10,11... | collective-permute-start | bytes 1228808 | tf_op jit(solution)/shard_map/ppermute | solution.py:263
  84.5 2.0 %collective-permute-start.17 = (bf16[80,2560]{1,0:T(8,128)(2,1)S(1)}, bf16[80,2560]{1,0:T(8,128)(2,1)S(1)}, u32[]{:S(2)}, u32[]{:S(2)}) collective-permute-start(bf16[80,2560]{1,0:T(8,128)(2,1)S(1)} %after.9.refs_1_), channel_id=1, source_target_pairs={{0,1},{1,0},{2,3},{3,2},{4,5},{5,4},{6,7},{7,6},{8,9},{9,8},{10,11... | collective-permute-start | bytes 1228808 | tf_op jit(solution)/shard_map/ppermute | solution.py:263
  89.2 23.0 %collective-permute-start.22 = (bf16[768,640]{1,0:T(8,128)(2,1)S(1)}, bf16[768,640]{1,0:T(8,128)(2,1)S(1)}, u32[]{:S(2)}, u32[]{:S(2)}) collective-permute-start(bf16[768,640]{1,0:T(8,128)(2,1)S(1)} %get-tuple-element.59), channel_id=1, source_target_pairs={{0,16},{8,24},{16,0},{24,8},{1,17},{9,25},{17,1},{25,9},{2,18},{10... | collective-permute-start | bytes 2949128 | tf_op jit(solution)/shard_map/ppermute | solution.py:266
  90.6 23.1 %collective-permute-start.20 = (bf16[768,640]{1,0:T(8,128)(2,1)S(1)}, bf16[768,640]{1,0:T(8,128)(2,1)S(1)}, u32[]{:S(2)}, u32[]{:S(2)}) collective-permute-start(bf16[768,640]{1,0:T(8,128)(2,1)S(1)} %get-tuple-element.55), channel_id=1, source_target_pairs={{0,8},{8,0},{16,24},{24,16},{1,9},{9,1},{17,25},{25,17},{2,10},{10... | collective-permute-start | bytes 2949128 | tf_op jit(solution)/shard_map/ppermute | solution.py:266
  91.8 4.9 %collective-permute-start.18 = (bf16[80,2560]{1,0:T(8,128)(2,1)S(1)}, bf16[80,2560]{1,0:T(8,128)(2,1)S(1)}, u32[]{:S(2)}, u32[]{:S(2)}) collective-permute-start(bf16[80,2560]{1,0:T(8,128)(2,1)S(1)} %get-tuple-element.52), channel_id=1, source_target_pairs={{0,1},{1,0},{2,3},{3,2},{4,5},{5,4},{6,7},{7,6},{8,9},{9,8},{10,11... | collective-permute-start | bytes 1228808 | tf_op jit(solution)/shard_map/ppermute | solution.py:263
  92.7 22.4 %collective-permute-start.14 = (bf16[80,2560]{1,0:T(8,128)(2,1)S(1)}, bf16[80,2560]{1,0:T(8,128)(2,1)S(1)}, u32[]{:S(2)}, u32[]{:S(2)}) collective-permute-start(bf16[80,2560]{1,0:T(8,128)(2,1)S(1)} %get-tuple-element.44.refs_9_), channel_id=1, source_target_pairs={{0,4},{1,5},{2,6},{3,7},{4,0},{5,1},{6,2},{7,3},{8,12},{9,13},{10,... | collective-permute-start | bytes 1228808 | tf_op jit(solution)/shard_map/ppermute | solution.py:260
  96.7 18.5 %collective-permute-start.13 = (bf16[80,2560]{1,0:T(8,128)(2,1)S(1)}, bf16[80,2560]{1,0:T(8,128)(2,1)S(1)}, u32[]{:S(2)}, u32[]{:S(2)}) collective-permute-start(bf16[80,2560]{1,0:T(8,128)(2,1)S(1)} %get-tuple-element.43), channel_id=1, source_target_pairs={{0,2},{1,3},{2,0},{3,1},{4,6},{5,7},{6,4},{7,5},{8,10},{9,11},{10,... | collective-permute-start | bytes 1228808 | tf_op jit(solution)/shard_map/ppermute | solution.py:260
  96.8 35.1 %collective-permute-start.19 = (bf16[80,2560]{1,0:T(8,128)(2,1)S(1)}, bf16[80,2560]{1,0:T(8,128)(2,1)S(1)}, u32[]{:S(2)}, u32[]{:S(2)}) collective-permute-start(bf16[80,2560]{1,0:T(8,128)(2,1)S(1)} %pair.3), channel_id=1, source_target_pairs={{0,6},{1,7},{2,4},{3,5},{4,2},{5,3},{6,0},{7,1},{8,14},{9,15},{10,... | collective-permute-start | bytes 1228808 | tf_op jit(solution)/shard_map/ppermute | solution.py:260
  112.4 21.4 %collective-permute-start.23 = (bf16[384,640]{1,0:T(8,128)(2,1)S(1)}, bf16[384,640]{1,0:T(8,128)(2,1)S(1)}, u32[]{:S(2)}, u32[]{:S(2)}) collective-permute-start(bf16[384,640]{1,0:T(8,128)(2,1)S(1)} %add_convert_fusion), channel_id=1, source_target_pairs={{0,8},{8,0},{16,24},{24,16},{1,9},{9,1},{17,25},{25,17},{2,10},{10... | collective-permute-start | bytes 1474568 | tf_op jit(solution)/shard_map/ppermute | solution.py:266
  113.9 21.0 %collective-permute-start.21 = (bf16[384,640]{1,0:T(8,128)(2,1)S(1)}, bf16[384,640]{1,0:T(8,128)(2,1)S(1)}, u32[]{:S(2)}, u32[]{:S(2)}) collective-permute-start(bf16[384,640]{1,0:T(8,128)(2,1)S(1)} %add_convert_fusion.1), channel_id=1, source_target_pairs={{0,16},{8,24},{16,0},{24,8},{1,17},{9,25},{17,1},{25,9},{2,18},{10... | collective-permute-start | bytes 1474568 | tf_op jit(solution)/shard_map/ppermute | solution.py:266
